TPU v7x, 256 devices: a whole 4x4x8 slice. The times are simulated.
256 devices in a mesh: span: 64 (over x, z, core), space: 4 (over y).
Axes of the slice: x: 4, y: 4, z: 8, core: 2. Of those that a mesh axis runs over, the one named last changes fastest.
Arguments:
- frames: bfloat16 [64, 4, 8, 128, 128], P('span', None, 'space'), may hold values from -200 to 200
- cotangent: bfloat16 [64, 4, 8, 128, 128], P('span', None, 'space'), may hold values from -6 to 6
- conv_weight: bfloat16 [3, 3, 3, 128, 128], replicated, may hold values from -0.109375 to 0.109375
- conv_bias: float32 [128], replicated, may hold values from -3 to 3
- norm_gain: float32 [128], replicated, may hold values from 0.1 to 1.9
- norm_shift: float32 [128], replicated, may hold values from -3 to 3
- clip_ids: int32 [64], replicated, may hold values from 0 to 8, never falling along the last dimension, each value on 1 to 32 neighbouring positions
Outputs:
- encoded: bfloat16 [64, 4, 8, 128, 128], P('span', None, 'space')
- frames_grad: bfloat16 [64, 4, 8, 128, 128], P('span', None, 'space')
- weight_grad: float32 [3, 3, 3, 128, 128], replicated
- bias_grad: float32 [128], replicated
- gain_grad: float32 [128], replicated
- shift_grad: float32 [128], replicated
Inputs may be any that keep to these rules, and one draw needn't show every extreme that they name: `clip_ids`: clip numbers never fall along the spans; every clip 0 to 8 holds 1 to 32 consecutive spans, one of them exactly 32.
All inputs are finite; a program needn't handle non-finite values.
Results may differ from a plain program's by a relative error of at most 0.0042.
Values may be sent and summed in bfloat16 or wider, within the bound.
A program may use at most 64 MiB of HBM per device.

v0:
```python
import math

import jax
import jax.numpy as jnp
from jax import lax
from jax.sharding import PartitionSpec as P

GROUPS = 32


epsilon = 1e-06


def padded_2(array, sides, width):
    for axis, dim in sides:
        peers, length = (lax.axis_size(axis), array.shape[dim])
        up = [(i, (i + 1) % peers) for i in range(peers - 1)]
        down = [(j, i) for i, j in up]
        last = lax.slice_in_dim(array, length - width, length, axis=dim)
        leading = lax.slice_in_dim(array, 0, width, axis=dim)
        before = lax.ppermute(last, axis, up)
        after = lax.ppermute(leading, axis, down)
        array = jnp.concatenate([before, array, after], axis=dim)
    return array


def passed_along(block, axis, distance):
    devices = range(lax.axis_size(axis))
    route = [(i - distance, i) for i in devices if i - distance in devices]
    return lax.ppermute(block, axis, route)


def conv_block(padded, kernel):
    frame_count = padded.shape[0] - 2
    row_count = padded.shape[1] - 2
    col_count = padded.shape[2] - 2
    channels = padded.shape[3]
    stacked = jnp.concatenate(
        [padded[:, :, col_tap : col_tap + col_count] for col_tap in range(3)], axis=-1
    )
    summed = jnp.zeros((frame_count * row_count * col_count, kernel.shape[-1]), jnp.float32)
    for time_tap in range(3):
        for row_tap in range(3):
            window = stacked[time_tap : time_tap + frame_count, row_tap : row_tap + row_count]
            window = window.reshape(frame_count * row_count * col_count, 3 * channels)
            summed = summed + jnp.dot(
                window, kernel[time_tap, row_tap], preferred_element_type=jnp.float32
            )
    return summed.reshape(frame_count, row_count, col_count, kernel.shape[-1])


def weight_block(padded, cot_block):
    frame_count, row_count, col_count, channels = cot_block.shape
    stacked = jnp.concatenate(
        [padded[:, :, col_tap : col_tap + col_count] for col_tap in range(3)], axis=-1
    )
    flat_cot = cot_block.reshape(-1, channels)
    pieces = []
    for time_tap in range(3):
        for row_tap in range(3):
            window = stacked[time_tap : time_tap + frame_count, row_tap : row_tap + row_count]
            window = window.reshape(-1, stacked.shape[-1])
            pieces.append(
                lax.dot_general(
                    window, flat_cot, (((0,), (0,)), ((), ())), preferred_element_type=jnp.float32
                )
            )
    return jnp.stack(pieces).reshape(3, 3, 3, stacked.shape[-1] // 3, channels)


def normalize(frame_block, center, inv_scale, norm_gain, norm_shift):
    channels = frame_block.shape[-1]
    grouped = frame_block.astype(jnp.float32).reshape(-1, GROUPS, channels // GROUPS)
    normed = ((grouped - center[None, :, None]) * inv_scale[None, :, None]).reshape(
        frame_block.shape
    )
    return (normed, normed * norm_gain + norm_shift)


def local(frames, cotangent, conv_weight, conv_bias, norm_gain, norm_shift, clip_ids):
    position = lax.axis_index("span")
    span_count = lax.axis_size("span")
    band_count = lax.axis_size("space")
    frame_count, row_count, col_count, channels = frames.shape[1:]
    per_group = channels // GROUPS
    clip_total = span_count // 8 + 1
    labels = jnp.arange(clip_total, dtype=jnp.int32)
    own_clip = clip_ids[position]
    own_clip_hot = (labels == own_clip).astype(jnp.float32)
    spans_of = jnp.sum((clip_ids[:, None] == labels[None, :]).astype(jnp.float32), axis=0)
    own_count = jnp.sum(own_clip_hot * spans_of) * (
        frame_count * row_count * band_count * col_count * per_group
    )
    earlier = clip_ids[jnp.maximum(position - 1, 0)]
    following = clip_ids[jnp.minimum(position + 1, span_count - 1)]
    starts = (position == 0) | (earlier != own_clip)
    same_next = (position < span_count - 1) & (following == own_clip)

    def pick(totals):
        return jnp.sum(own_clip_hot[:, None] * totals, axis=0) / own_count

    local_frames = frames[0]
    grouped = local_frames.astype(jnp.float32).reshape(-1, GROUPS, per_group)
    local_sums = jnp.sum(grouped, axis=(0, 2))
    totals = lax.psum(own_clip_hot[:, None] * local_sums[None, :], ("span", "space"))
    group_mean = pick(totals)
    centered = grouped - group_mean[None, :, None]
    square_totals = lax.psum(
        own_clip_hot[:, None] * jnp.sum(centered * centered, axis=(0, 2))[None, :],
        ("span", "space"),
    )
    variance = pick(square_totals)
    inverse_std = lax.rsqrt(variance + epsilon)
    normed, lifted = normalize(local_frames, group_mean, inverse_std, norm_gain, norm_shift)
    active = jax.nn.silu(lifted).astype(jnp.bfloat16)
    active_rows = padded_2(active, (("space", 1),), 1)
    last_frames = passed_along(active_rows[frame_count - 2 :], "span", 1)
    first_copy = jnp.concatenate([active_rows[0:1], active_rows[0:1]], axis=0)
    active_ext = jnp.concatenate([jnp.where(starts, first_copy, last_frames), active_rows], axis=0)
    col_pad = ((0, 0), (0, 0), (1, 1), (0, 0))
    padded = jnp.pad(active_ext, col_pad)
    kernel = conv_weight.reshape(3, 3, 3 * channels, channels)
    encoded = (conv_block(padded, kernel) + conv_bias).astype(jnp.bfloat16)
    cot_rows = padded_2(cotangent[0], (("space", 1),), 1)
    blank_frames = jnp.zeros((2,) + cot_rows.shape[1:], jnp.bfloat16)
    cot_padded = jnp.pad(jnp.concatenate([blank_frames, cot_rows, blank_frames], axis=0), col_pad)
    flipped = jnp.swapaxes(conv_weight[::-1, ::-1, ::-1], 3, 4).reshape(
        3, 3, 3 * channels, channels
    )
    adjoint_ext = conv_block(cot_padded, flipped)
    adjoint = adjoint_ext[2:]
    returned = passed_along(adjoint_ext[0:2], "span", -1)
    adjoint = jnp.concatenate(
        [
            adjoint[: frame_count - 2],
            adjoint[frame_count - 2 :] + jnp.where(same_next, returned, 0.0),
        ],
        axis=0,
    )
    start_term = jnp.where(starts, adjoint_ext[0] + adjoint_ext[1], 0.0)
    adjoint = jnp.concatenate([adjoint[0:1] + start_term[None], adjoint[1:]], axis=0)
    sigmoid_val = jax.nn.sigmoid(lifted)
    pre_grad = adjoint * sigmoid_val * (1.0 + lifted * (1.0 - sigmoid_val))
    gain_terms = jnp.sum((pre_grad * normed).reshape(-1, channels), axis=0)
    shift_terms = jnp.sum(pre_grad.reshape(-1, channels), axis=0)
    scaled = (pre_grad * norm_gain).reshape(-1, GROUPS, per_group)
    normed_grouped = normed.reshape(-1, GROUPS, per_group)
    first_totals, second_totals = lax.psum(
        (
            own_clip_hot[:, None] * jnp.sum(scaled, axis=(0, 2))[None, :],
            own_clip_hot[:, None] * jnp.sum(scaled * normed_grouped, axis=(0, 2))[None, :],
        ),
        ("span", "space"),
    )
    first_mean = pick(first_totals)
    second_mean = pick(second_totals)
    result = inverse_std[None, :, None] * (
        scaled - first_mean[None, :, None] - normed_grouped * second_mean[None, :, None]
    )
    frames_grad = result.reshape(local_frames.shape).astype(jnp.bfloat16)
    weight_terms = weight_block(padded, cotangent[0])
    bias_terms = jnp.sum(cotangent[0].astype(jnp.float32).reshape(-1, channels), axis=0)
    weight_sum, bias_sum, gain_sum, shift_sum = lax.psum(
        (weight_terms, bias_terms, gain_terms, shift_terms), ("span", "space")
    )
    factor = 1.0 / math.sqrt(span_count * frame_count * row_count * band_count * col_count)
    return (
        encoded[None],
        frames_grad[None],
        weight_sum * factor,
        bias_sum * factor,
        gain_sum * factor,
        shift_sum * factor,
    )


def solution(mesh):
    placed = (
        P("span", None, "space", None, None),
        P("span", None, "space", None, None),
        P(),
        P(),
        P(),
        P(),
        P(),
    )
    return jax.shard_map(
        local,
        mesh=mesh,
        in_specs=placed,
        out_specs=(
            P("span", None, "space", None, None),
            P("span", None, "space", None, None),
            P(),
            P(),
            P(),
            P(),
        ),
        check_vma=False,
    )
```

profile of v0, /device:TPU:1, one launch (start us, length us, event | category | flops | bytes accessed | tf_op | source)
XLA Modules:
  0.0 561.8 jit_solution(10502740629623164465)
XLA Ops:
  7.2 1.0 fusion.94
  8.2 4.0 collective-permute-start.3
  12.3 1.3 collective-permute-start.4
  13.6 2.0 copy.14
  15.9 0.6 fusion.96
  16.5 0.6 compare_convert_fusion
  17.6 81.4 %psum.56 = f32[9,32]{1,0:T(8,128)S(1)} all-reduce(f32[9,32]{1,0:T(8,128)S(1)} %broadcast_multiply_fusion.4), channel_id=1, replica_groups=mesh['span'=64,'space'=4] {'span','space'}, use_global_device_ids=true, to_apply=%region_2.0 | all-reduce | flops 288 | bytes 2304 | tf_op jit(solution)/shard_map/psum | solution.py:105
  99.0 1.2 fusion.88
  101.6 72.7 %psum.57 = f32[9,32]{1,0:T(8,128)S(1)} all-reduce(f32[9,32]{1,0:T(8,128)S(1)} %broadcast_multiply_fusion.3), channel_id=1, replica_groups=mesh['span'=64,'space'=4] {'span','space'}, use_global_device_ids=true, to_apply=%region_8.9 | all-reduce | flops 288 | bytes 2304 | tf_op jit(solution)/shard_map/psum | solution.py:108
  174.7 0.6 fusion.91
  175.9 2.0 fusion.89
  181.7 0.6 fusion.6
  182.4 2.6 collective-permute-start.5
  188.0 2.7 collective-permute-done.5
  191.7 2.2 collective-permute-start
  193.9 1.3 collective-permute-start.1
  195.3 76.8 %all-reduce.2 = (f32[9,32]{1,0:T(8,128)S(1)}, f32[9,32]{1,0:T(8,128)S(1)}, f32[128]{0:T(128)S(1)}, f32[128]{0:T(128)S(1)}, f32[128]{0:T(128)S(1)}) all-reduce(f32[9,32]{1,0:T(8,128)S(1)} %get-tuple-element.49, f32[9,32]{1,0:T(8,128)S(1)} %get-tuple-element.48, ...), channel_id=1, replica_groups=mesh['span'=64,'space'=4] {'span','space'}, use_global_device_ids=true, to_apply=%region_12.13 | all-reduce | flops 960 | bytes 7680 | tf_op jit(solution)/shard_map/psum | solution.py:148
  272.6 1.1 fusion.51
  274.2 2.7 collective-permute-start.2
  277.4 2.6 collective-permute-done.2
  281.1 1.2 fusion.90
  284.0 1.2 fusion.85
  285.1 1.2 fusion.84
  286.7 1.2 fusion.83
  288.3 1.2 fusion.82
  289.9 1.2 fusion.81
  291.5 1.2 fusion.80
  293.1 1.2 copy-done.3
  296.0 1.5 fusion.15
  297.5 0.8 add_convert_fusion
  298.2 253.9 %all-reduce.5.cloned.1.call-done = f32[3,3,3,128,128]{4,3,2,1,0:T(8,128)} async-done(((f32[3,3,3,128,128]{4,3,2,1,0:T(8,128)}), f32[3,3,3,128,128]{4,3,2,1,0:T(8,128)}) %all-reduce.5.cloned.1.call-update) | async-done | bytes 1769488 | tf_op jit(solution)/shard_map/psum | solution.py:163
  552.1 2.9 broadcast_multiply_fusion
  (98 shorter events, 15.5 us)
Async XLA Ops:
  7.2 544.9 %all-reduce.5.cloned.1.call-start = ((), (), s32[]{:S(2)}) async-start(), calls=%async_computation | async-start | bytes 3538944 | tf_op jit(solution)/shard_map/psum | solution.py:163
  8.2 166.2 %collective-permute-start.3 = (bf16[4,1,128,128]{3,2,1,0:T(8,128)(2,1)S(1)}, bf16[4,1,128,128]{3,2,1,0:T(8,128)(2,1)S(1)}, u32[]{:S(2)}, u32[]{:S(2)}) collective-permute-start(bf16[4,1,128,128]{3,2,1,0:T(8,128)(2,1)S(1)} %get-tuple-element.44), channel_id=1, source_target_pairs={{0,1},{1,2},{2,3},{4,5},{5,6},{6,7},{8,9},{9,10},{10,11},{12,13},{... | collective-permute-start | bytes 393224 | tf_op jit(solution)/shard_map/ppermute | solution.py:21
  12.3 162.1 %collective-permute-start.4 = (bf16[4,1,128,128]{3,2,1,0:T(8,128)(2,1)S(1)}, bf16[4,1,128,128]{3,2,1,0:T(8,128)(2,1)S(1)}, u32[]{:S(2)}, u32[]{:S(2)}) collective-permute-start(bf16[4,1,128,128]{3,2,1,0:T(8,128)(2,1)S(1)} %get-tuple-element.45), channel_id=1, source_target_pairs={{1,0},{2,1},{3,2},{5,4},{6,5},{7,6},{9,8},{10,9},{11,10},{13,12},{... | collective-permute-start | bytes 393224 | tf_op jit(solution)/shard_map/ppermute | solution.py:22
  13.6 2.2 copy-start.10
  13.6 3.5 copy-start.1
  15.6 158.8 %copy-start = (bf16[1,4,2,128,128]{4,3,2,1,0:T(8,128)(2,1)S(1)}, bf16[1,4,2,128,128]{4,3,2,1,0:T(8,128)(2,1)}, u32[]{:S(2)}) copy-start(bf16[1,4,2,128,128]{4,3,2,1,0:T(8,128)(2,1)} %param.8) | copy-start | bytes 786436
  182.3 8.4 %copy-start.9 = (f32[128]{0:T(128)S(1)}, f32[128]{0:T(128)}, u32[]{:S(2)}) copy-start(f32[128]{0:T(128)} %param.11) | copy-start | bytes 1540
  182.3 8.4 %copy-start.11 = (f32[128]{0:T(128)S(1)}, f32[128]{0:T(128)}, u32[]{:S(2)}) copy-start(f32[128]{0:T(128)} %param.12) | copy-start | bytes 1540
  182.4 8.3 %collective-permute-start.5 = (f32[2,2,128,128]{3,2,1,0:T(8,128)S(1)}, f32[2,2,128,128]{3,2,1,0:T(8,128)S(1)}, u32[]{:S(2)}, u32[]{:S(2)}) collective-permute-start(f32[2,2,128,128]{3,2,1,0:T(8,128)S(1)} %bitcast.265), channel_id=1, source_target_pairs={{4,0},{8,4},{12,8},{16,12},{20,16},{24,20},{28,24},{32,28},{36,32}... | collective-permute-start | bytes 786440 | tf_op jit(solution)/shard_map/ppermute | solution.py:30
  191.7 82.4 %collective-permute-start = (bf16[4,1,128,128]{3,2,1,0:T(8,128)(2,1)S(1)}, bf16[4,1,128,128]{3,2,1,0:T(8,128)(2,1)S(1)}, u32[]{:S(2)}, u32[]{:S(2)}) collective-permute-start(bf16[4,1,128,128]{3,2,1,0:T(8,128)(2,1)S(1)} %get-tuple-element.46), channel_id=1, source_target_pairs={{0,1},{1,2},{2,3},{4,5},{5,6},{6,7},{8,9},{9,10},{10,11},{12,13},{... | collective-permute-start | bytes 393224 | tf_op jit(solution)/shard_map/ppermute | solution.py:21
  193.9 80.2 %collective-permute-start.1 = (bf16[4,1,128,128]{3,2,1,0:T(8,128)(2,1)S(1)}, bf16[4,1,128,128]{3,2,1,0:T(8,128)(2,1)S(1)}, u32[]{:S(2)}, u32[]{:S(2)}) collective-permute-start(bf16[4,1,128,128]{3,2,1,0:T(8,128)(2,1)S(1)} %get-tuple-element.47), channel_id=1, source_target_pairs={{1,0},{2,1},{3,2},{5,4},{6,5},{7,6},{9,8},{10,9},{11,10},{13,12},{... | collective-permute-start | bytes 393224 | tf_op jit(solution)/shard_map/ppermute | solution.py:22
  274.2 5.8 %collective-permute-start.2 = (bf16[2,4,128,128]{3,2,1,0:T(8,128)(2,1)S(1)}, bf16[2,4,128,128]{3,2,1,0:T(8,128)(2,1)S(1)}, u32[]{:S(2)}, u32[]{:S(2)}) collective-permute-start(bf16[2,4,128,128]{3,2,1,0:T(8,128)(2,1)S(1)} %pad_maximum_fusion.3), channel_id=1, source_target_pairs={{0,4},{4,8},{8,12},{12,16},{16,20},{20,24},{24,28},{28,32},{32,36}... | collective-permute-start | bytes 786440 | tf_op jit(solution)/shard_map/ppermute | solution.py:30
  282.7 1.3 copy-start.2
  293.1 1.2 copy-start.3
  294.3 1.0 copy-start.4
  294.3 1.2 copy-start.5
  294.3 1.3 copy-start.6
  294.3 1.5 copy-start.7
  294.3 1.6 copy-start.8
  296.0 1.5 copy-start.12
Sparse Core Ops, SparseCore 0:
  294.4 257.6 all-reduce.4
where the time goes:
time: 563 us; the launch traced here: 562 us
  waiting for transfers between devices  259 us (46%)
  blocking collectives  231 us (41%)
  between operations  17.9 us (3%)
  matrix products  17.2 us (3%)
  starting transfers between devices  14.1 us (3%)
  local copies, waits for them, and re-layouts  11.3 us (2%)
  other arithmetic  11.2 us (2%)
    psum x1, waiting for transfers between devices, local(): lax.psum((weight_terms, bias_terms, gain_terms, shift_terms), ('span', 's...  254 us
    psum x1, blocking collectives, local(): lax.psum(own_clip_hot[:, None] * local_sums[None, :], ('span', 'space'))  81.4 us
    psum x1, blocking collectives, local(): lax.psum((own_clip_hot[:, None] * jnp.sum(scaled, axis=(0, 2))[None, :],...  76.8 us
    psum x1, blocking collectives, local(): lax.psum(own_clip_hot[:, None] * jnp.sum(centered * centered, axis=(0, 2)...  72.7 us
    dot_general x18, matrix products, conv_block(): jnp.dot(window, kernel[time_tap, row_tap], preferred_element_type=jnp.flo...  13.6 us
  transfers between devices with their start and end apart: 7, of which 3 were waited for; matrix products, arithmetic and copies ran while one was open for 2% of the time, Pallas kernels for 0%

commit v1 on v0

v1 whole, which is shorter than its diff:
```python
import functools
import math

import jax
import jax.numpy as jnp
from jax import lax
from jax.experimental import pallas as pl
from jax.experimental.pallas import tpu as pltpu
from jax.sharding import PartitionSpec as P

MESH = pl.DeviceIdType.MESH
F32 = jnp.float32
BF16 = jnp.bfloat16

NX, NY, NZ, NC = 4, 4, 8, 2
SPANS = NX * NZ * NC
PLANE = NX * NY
LINE = NZ * NC
C = 128
PER_GROUP = 4
FR = 4
RB = 2
W = 128
EPSILON = 1e-06
POSITIONS = SPANS * FR * RB * NY * W
PER_DEVICE = FR * RB * W * PER_GROUP
PER_SPAN = PER_DEVICE * NY
TAP_ROWS = 27 * C
HALF = TAP_ROWS // 2
CHUNK = 112
REGION = PLANE * CHUNK

(S_P1, S_P2, S_FH, S_CH, S_CORE, S_XY, S_Z, S_GXY, S_GCORE, S_Q1, S_Q2) = range(11)


def group_sum(v):
    lane = lax.broadcasted_iota(jnp.int32, v.shape, 1)
    pair = v + jnp.where(lane % 2 == 0, pltpu.roll(v, 127, axis=1), pltpu.roll(v, 1, axis=1))
    return pair + jnp.where(lane % 4 < 2, pltpu.roll(pair, 126, axis=1), pltpu.roll(pair, 2, axis=1))


def distance(d, n):
    return min(d, n - d)


PLANE_OFFS = sorted(
    [(a, b) for a in range(NX) for b in range(NY) if (a, b) != (0, 0)],
    key=lambda o: -(distance(o[0], NX) + distance(o[1], NY)),
)
LINE_OFFS = sorted(
    [(a, b) for a in range(NZ) for b in range(NC) if (a, b) != (0, 0)],
    key=lambda o: -(4 * distance(o[0], NZ) + o[1]),
)
Z_OFFS = sorted(range(1, NZ), key=lambda o: -distance(o, NZ))


def wait_for(ref, sem):
    pltpu.make_async_copy(ref, ref, sem).wait()


def shifted(v, back):
    row = lax.broadcasted_iota(jnp.int32, v.shape, 0)
    if back:
        return jnp.where(row == 0, 0.0, pltpu.roll(v, 1, axis=0))
    return jnp.where(row == W - 1, 0.0, pltpu.roll(v, W - 1, axis=0))


def rows_sum(v):
    return jnp.sum(v.reshape(W // 8, 8, C), axis=0)


def kernel(
    frames, cot, wt, bias, gain, shift, clip,
    enc_out, fg_out, wg_out, small_out,
    fp_buf, cp_buf, act, act_t, act_st, cot_st, wcat,
    p1_src, p1, p2_src, p2, q1_src, q1, q2_src, q2, masks,
    grads, r_core, s_xy, r_xy, r_z, t_xy, t_core, acc,
    send, recv,
):
    span = lax.axis_index("span")
    y = lax.axis_index("space")
    x = lax.div(span, LINE)
    line = lax.rem(span, LINE)
    z = lax.div(line, NC)
    c = lax.rem(span, NC)
    plane = x * NY + y

    def in_plane(o):
        return (lax.rem(x + o[0], NX) * LINE + line, lax.rem(y + o[1], NY))

    def in_line(o):
        return (x * LINE + lax.rem(z + o[0], NZ) * NC + lax.rem(c + o[1], NC), y)

    def beside(ds, dy):
        return (lax.rem(span + ds + SPANS, SPANS), lax.rem(y + dy + NY, NY))

    def push(src, dst, which, device):
        pltpu.make_async_remote_copy(
            src_ref=src, dst_ref=dst, send_sem=send.at[which], recv_sem=recv.at[which],
            device_id=device, device_id_type=MESH,
        ).start()

    barrier = pltpu.get_barrier_semaphore()
    partners = [in_plane(o) for o in PLANE_OFFS] + [in_line(o) for o in LINE_OFFS]
    partners += [beside(ds, dy) for ds in (-1, 1) for dy in (-1, 0, 1)]
    for device in partners:
        pl.semaphore_signal(barrier, inc=1, device_id=device, device_id_type=MESH)

    def add_rows(j, total):
        return total + rows_sum(frames[0, j // RB, j % RB].astype(F32))

    total = lax.fori_loop(0, FR * RB, add_rows, jnp.zeros((8, C), F32))
    mean_here = group_sum(jnp.sum(total, axis=0, keepdims=True)) * (1.0 / PER_DEVICE)

    def add_squares(j, total):
        v = frames[0, j // RB, j % RB].astype(F32) - mean_here
        return total + rows_sum(v * v)

    total = lax.fori_loop(0, FR * RB, add_squares, jnp.zeros((8, C), F32))
    squares_here = group_sum(jnp.sum(total, axis=0, keepdims=True))
    block = jnp.concatenate([mean_here, squares_here, jnp.zeros((6, C), F32)], axis=0)
    p1_src[...] = block
    p1[plane] = block

    pl.semaphore_wait(barrier, len(partners))
    for o in PLANE_OFFS:
        push(p1_src, p1.at[plane], S_P1, in_plane(o))
    push(frames.at[0, :, 1], fp_buf.at[pl.ds(2, FR), 0], S_FH, beside(0, 1))
    push(frames.at[0, :, 0], fp_buf.at[pl.ds(2, FR), 3], S_FH, beside(0, -1))
    push(frames.at[0, pl.ds(2, 2)], fp_buf.at[pl.ds(0, 2), pl.ds(1, RB)], S_FH, beside(1, 0))
    push(frames.at[0, pl.ds(2, 2), 1], fp_buf.at[pl.ds(0, 2), 0], S_FH, beside(1, 1))
    push(frames.at[0, pl.ds(2, 2), 0], fp_buf.at[pl.ds(0, 2), 3], S_FH, beside(1, -1))

    own = clip[span]
    before = clip[lax.rem(span + SPANS - 1, SPANS)]
    after = clip[lax.rem(span + 1, SPANS)]
    starts = jnp.where((span == 0) | (before != own), 1.0, 0.0).astype(F32)
    same_next = jnp.where((span < SPANS - 1) & (after == own), 1.0, 0.0).astype(F32)
    above = jnp.where(y > 0, 1.0, 0.0).astype(F32)
    below = jnp.where(y < NY - 1, 1.0, 0.0).astype(F32)

    sub = lax.broadcasted_iota(jnp.int32, (8, C), 0)

    def fill_masks(k, count):
        block = jnp.zeros((8, C), F32)
        for a in range(NX):
            member = jnp.where(clip[a * LINE + k] == own, 1.0, 0.0).astype(F32)
            block = block + jnp.where(sub % 4 == a, member, 0.0)
            count = count + member
        masks[k] = block
        return count

    spans_here = lax.fori_loop(0, LINE, fill_masks, jnp.float32(0.0))
    spans_row = jnp.zeros((1, C), F32) + spans_here
    inv_count = 1.0 / (spans_row * PER_SPAN)

    def stack_cot(v, f, r):
        cot_st[f, r, :, 0:C] = shifted(v, False).astype(BF16)
        cot_st[f, r, :, C:2 * C] = v.astype(BF16)
        cot_st[f, r, :, 2 * C:3 * C] = shifted(v, True).astype(BF16)

    def stack_own(f, total):
        for r in range(RB):
            v = cot[0, f, r].astype(F32)
            total = total + rows_sum(v)
            stack_cot(v, f, r + 1)
            fp_buf[f + 2, r + 1] = frames[0, f, r]
        return total

    bias_terms = lax.fori_loop(0, FR, stack_own, jnp.zeros((8, C), F32))
    bias_terms = jnp.sum(bias_terms, axis=0, keepdims=True)

    wait_for(p1.at[pl.ds(0, PLANE - 1)], recv.at[S_P1])
    mean_rows, square_rows = [], []
    for a in range(NX):
        parts = [p1[a * NY + b] for b in range(NY)]
        summed = parts[0] + parts[1] + parts[2] + parts[3]
        mean = summed[0:1] * (1.0 / NY)
        spread = sum((q[0:1] - mean) * (q[0:1] - mean) for q in parts)
        mean_rows.append(mean)
        square_rows.append(summed[1:2] + PER_DEVICE * spread)
    block = jnp.concatenate(mean_rows + square_rows, axis=0)
    p2_src[...] = block
    p2[line] = block
    for o in LINE_OFFS:
        push(p2_src, p2.at[line], S_P2, in_line(o))
    push(cot.at[0, :, 1], cp_buf.at[pl.ds(0, FR), 0], S_CH, beside(0, 1))
    push(cot.at[0, :, 0], cp_buf.at[pl.ds(0, FR), 3], S_CH, beside(0, -1))
    push(cot.at[0, pl.ds(0, 2)], cp_buf.at[pl.ds(4, 2), pl.ds(1, RB)], S_CH, beside(-1, 0))
    push(cot.at[0, pl.ds(0, 2), 1], cp_buf.at[pl.ds(4, 2), 0], S_CH, beside(-1, 1))
    push(cot.at[0, pl.ds(0, 2), 0], cp_buf.at[pl.ds(4, 2), 3], S_CH, beside(-1, -1))

    def widen(t, carry):
        for ds in range(3):
            wcat[t, :, ds * C:(ds + 1) * C] = wt[t, pl.ds(ds * C, C)]
        return carry

    lax.fori_loop(0, 9, widen, 0)

    wait_for(fp_buf.at[pl.ds(0, 4)], recv.at[S_FH])

    def carry_rows(r, carry):
        first = fp_buf[2, r].astype(F32) * starts
        for f in range(2):
            fp_buf[f, r] = (first + fp_buf[f, r].astype(F32) * (1.0 - starts)).astype(BF16)
        return carry

    lax.fori_loop(0, RB + 2, carry_rows, 0)

    wait_for(p2.at[pl.ds(0, LINE - 1)], recv.at[S_P2])
    summed = jnp.zeros((8, C), F32)
    for k in range(LINE):
        summed = summed + p2[k] * masks[k]
    mean = jnp.sum(summed[0:4], axis=0, keepdims=True) / spans_row
    squares = jnp.sum(summed[4:8], axis=0, keepdims=True)
    spread = jnp.zeros((8, C), F32)
    for k in range(LINE):
        off = p2[k] - mean
        spread = spread + off * off * masks[k]
    squares = squares + PER_SPAN * jnp.sum(spread[0:4], axis=0, keepdims=True)
    inverse_std = lax.rsqrt(squares * inv_count + EPSILON)
    gain_row = gain[...]
    shift_row = shift[...]
    lift = inverse_std * gain_row

    def activate(f, carry):
        for r in range(RB + 2):
            lifted = (fp_buf[f, r].astype(F32) - mean) * lift + shift_row
            a = lifted / (1.0 + jnp.exp(-lifted))
            if r == 0:
                a = a * above
            if r == RB + 1:
                a = a * below
            act[f, r] = a.astype(BF16)
            flat = a.T.astype(BF16)
            for k in range(RB):
                dr = r - k
                if 0 <= dr < 3:
                    act_t[f, dr * C:(dr + 1) * C, k * W:(k + 1) * W] = flat
        return carry

    lax.fori_loop(0, FR + 2, activate, 0)

    def tap_grad(t, carry):
        left = jnp.concatenate([act_t[t + f] for f in range(FR)], axis=1)
        right = cot_st[0:FR, 1:1 + RB].reshape(FR * RB * W, 3 * C)
        g = jnp.dot(left, right, preferred_element_type=F32)
        for dr in range(3):
            for ds in range(3):
                piece = g[dr * C:(dr + 1) * C, ds * C:(ds + 1) * C].astype(BF16)
                grads[pl.ds(pl.multiple_of(t * 9 * C + (dr * 3 + ds) * C, C), C)] = piece
        return carry

    lax.fori_loop(0, 3, tap_grad, 0)
    other = pl.multiple_of((1 - c) * HALF, 64)
    push(grads.at[pl.ds(other, HALF)], r_core, S_CORE, in_line((0, 1)))
    s_xy[HALF:REGION] = jnp.zeros((REGION - HALF, C), BF16)
    wait_for(r_core, recv.at[S_CORE])
    mine = pl.multiple_of(c * HALF, 64)

    def add_core(k, carry):
        at = pl.multiple_of(k * 64, 64)
        own_part = grads[pl.ds(pl.multiple_of(mine + at, 64), 64)].astype(F32)
        s_xy[pl.ds(at, 64)] = (own_part + r_core[pl.ds(at, 64)].astype(F32)).astype(BF16)
        return carry

    lax.fori_loop(0, HALF // 64, add_core, 0)
    for o in PLANE_OFFS:
        px, py = lax.rem(x + o[0], NX), lax.rem(y + o[1], NY)
        at = pl.multiple_of((px * NY + py) * CHUNK, 16)
        push(s_xy.at[pl.ds(at, CHUNK)], r_xy.at[plane], S_XY, in_plane(o))
    r_xy[plane] = s_xy[pl.ds(pl.multiple_of(plane * CHUNK, 16), CHUNK)]

    wait_for(cp_buf.at[pl.ds(0, 4)], recv.at[S_CH])

    def stack_sides(f, carry):
        stack_cot(cp_buf[f, 0].astype(F32) * above, f, 0)
        stack_cot(cp_buf[f, 3].astype(F32) * below, f, 3)
        return carry

    lax.fori_loop(0, FR, stack_sides, 0)

    def stack_next(f, carry):
        for r in range(RB + 2):
            edge = above if r == 0 else below if r == RB + 1 else 1.0
            stack_cot(cp_buf[f, r].astype(F32) * (same_next * edge), f, r)
        return carry

    lax.fori_loop(FR, FR + 2, stack_next, 0)

    acc[...] = jnp.zeros_like(acc)

    def contract(window, k):
        return lax.dot_general(
            window, k, (((1,), (1,)), ((), ())), preferred_element_type=F32
        )

    def adjoint_tap(t, carry):
        dt, dr = lax.div(t, 3), lax.rem(t, 3)
        window = cot_st[pl.ds(2 - dt, FR), pl.ds(2 - dr, RB)].reshape(FR * RB * W, 3 * C)
        acc[...] += contract(window, wcat[t])
        return carry

    lax.fori_loop(0, 9, adjoint_tap, 0)

    def front_tap(dr, carry):
        zero = cot_st[0, pl.ds(2 - dr, RB)].reshape(RB * W, 3 * C)
        one = cot_st[1, pl.ds(2 - dr, RB)].reshape(RB * W, 3 * C)
        front = contract(zero, wcat[dr]) + contract(one, wcat[dr]) + contract(zero, wcat[dr + 3])
        acc[0:RB * W] += starts * front
        return carry

    lax.fori_loop(0, 3, front_tap, 0)

    def pre_grads(j, sums):
        at = pl.ds(pl.multiple_of(j * W, W), W)
        normed = (frames[0, j // RB, j % RB].astype(F32) - mean) * inverse_std
        lifted = normed * gain_row + shift_row
        s = 1.0 / (1.0 + jnp.exp(-lifted))
        pre = acc[at] * s * (1.0 + lifted * (1.0 - s))
        acc[at] = pre
        return sums[0] + rows_sum(pre), sums[1] + rows_sum(pre * normed)

    zero = jnp.zeros((8, C), F32)
    shift_terms, gain_terms = lax.fori_loop(0, FR * RB, pre_grads, (zero, zero))
    shift_terms = jnp.sum(shift_terms, axis=0, keepdims=True)
    gain_terms = jnp.sum(gain_terms, axis=0, keepdims=True)
    block = jnp.concatenate([shift_terms, gain_terms, bias_terms, jnp.zeros((5, C), F32)], axis=0)
    q1_src[...] = block
    q1[plane] = block
    for o in PLANE_OFFS:
        push(q1_src, q1.at[plane], S_Q1, in_plane(o))

    wait_for(r_xy.at[pl.ds(0, PLANE - 1)], recv.at[S_XY])
    total = r_xy[0].astype(F32)
    for k in range(1, PLANE):
        total = total + r_xy[k].astype(F32)
    r_z[z] = total.astype(BF16)
    for o in Z_OFFS:
        push(r_z.at[z], r_z.at[z], S_Z, in_line((o, 0)))

    def stack_act(f, carry):
        for r in range(RB + 2):
            v = act[f, r].astype(F32)
            act_st[f, r, :, 0:C] = shifted(v, True).astype(BF16)
            act_st[f, r, :, C:2 * C] = act[f, r]
            act_st[f, r, :, 2 * C:3 * C] = shifted(v, False).astype(BF16)
        return carry

    lax.fori_loop(0, FR + 2, stack_act, 0)

    wait_for(q1.at[pl.ds(0, PLANE - 1)], recv.at[S_Q1])
    rows = []
    bias_sum = jnp.zeros((1, C), F32)
    for a in range(NX):
        summed = q1[a * NY] + q1[a * NY + 1] + q1[a * NY + 2] + q1[a * NY + 3]
        rows.append(summed)
        bias_sum = bias_sum + summed[2:3]
    block = jnp.concatenate(
        [q[0:1] for q in rows] + [q[1:2] for q in rows] + [bias_sum, jnp.zeros((7, C), F32)], axis=0
    )
    q2_src[...] = block
    q2[line] = block
    for o in LINE_OFFS:
        push(q2_src, q2.at[line], S_Q2, in_line(o))

    wait_for(r_z.at[pl.ds(0, NZ - 1)], recv.at[S_Z])
    total = r_z[0].astype(F32)
    for k in range(1, NZ):
        total = total + r_z[k].astype(F32)
    t_xy[plane] = total.astype(BF16)
    for o in PLANE_OFFS:
        push(t_xy.at[plane], t_xy.at[plane], S_GXY, in_plane(o))


    wait_for(q2.at[pl.ds(0, LINE - 1)], recv.at[S_Q2])
    summed = jnp.zeros((8, C), F32)
    whole = jnp.zeros((16, C), F32)
    for k in range(LINE):
        part = q2[k]
        whole = whole + part
        summed = summed + part[0:8] * masks[k]
    first_mean = group_sum(jnp.sum(summed[0:4], axis=0, keepdims=True) * gain_row) * inv_count
    second_mean = group_sum(jnp.sum(summed[4:8], axis=0, keepdims=True) * gain_row) * inv_count
    factor = 1.0 / math.sqrt(POSITIONS)
    small_out[...] = jnp.concatenate(
        [
            whole[8:9],
            jnp.sum(whole[4:8], axis=0, keepdims=True),
            jnp.sum(whole[0:4], axis=0, keepdims=True),
            jnp.zeros((5, C), F32),
        ],
        axis=0,
    ) * factor

    def frame_grads(j, carry):
        at = pl.ds(pl.multiple_of(j * W, W), W)
        normed = (frames[0, j // RB, j % RB].astype(F32) - mean) * inverse_std
        result = inverse_std * (acc[at] * gain_row - first_mean - normed * second_mean)
        fg_out[0, j // RB, j % RB] = result.astype(BF16)
        return carry

    lax.fori_loop(0, FR * RB, frame_grads, 0)

    acc[...] = jnp.zeros_like(acc) + bias[...]

    def forward_tap(t, carry):
        dt, dr = lax.div(t, 3), lax.rem(t, 3)
        window = act_st[pl.ds(dt, FR), pl.ds(dr, RB)].reshape(FR * RB * W, 3 * C)
        acc[...] += jnp.dot(window, wt[t], preferred_element_type=F32)
        return carry

    lax.fori_loop(0, 9, forward_tap, 0)
    enc_out[0] = acc[...].astype(BF16).reshape(FR, RB, W, C)

    wait_for(t_xy.at[pl.ds(0, PLANE - 1)], recv.at[S_GXY])
    push(t_xy, t_core, S_GCORE, in_line((0, 1)))

    def write(src, base):
        at = pl.multiple_of(base, 64)
        wg_out[pl.ds(at, HALF)] = src[...].reshape(REGION, C)[0:HALF]

    write(t_xy, c * HALF)
    wait_for(t_core, recv.at[S_GCORE])
    write(t_core, (1 - c) * HALF)

    wait_for(p1.at[pl.ds(0, PLANE - 1)], send.at[S_P1])
    wait_for(p2.at[pl.ds(0, LINE - 1)], send.at[S_P2])
    wait_for(fp_buf.at[pl.ds(0, 4)], send.at[S_FH])
    wait_for(cp_buf.at[pl.ds(0, 4)], send.at[S_CH])
    wait_for(r_core, send.at[S_CORE])
    wait_for(r_xy.at[pl.ds(0, PLANE - 1)], send.at[S_XY])
    wait_for(r_z.at[pl.ds(0, NZ - 1)], send.at[S_Z])
    wait_for(t_xy.at[pl.ds(0, PLANE - 1)], send.at[S_GXY])
    wait_for(t_core, send.at[S_GCORE])
    wait_for(q1.at[pl.ds(0, PLANE - 1)], send.at[S_Q1])
    wait_for(q2.at[pl.ds(0, LINE - 1)], send.at[S_Q2])


def local(frames, cotangent, conv_weight, conv_bias, norm_gain, norm_shift, clip_ids):
    vmem = pl.BlockSpec(memory_space=pltpu.VMEM)
    smem = pl.BlockSpec(memory_space=pltpu.SMEM)
    enc, fg, wg, small = pl.pallas_call(
        kernel,
        out_shape=(
            jax.ShapeDtypeStruct(frames.shape, BF16),
            jax.ShapeDtypeStruct(frames.shape, BF16),
            jax.ShapeDtypeStruct((TAP_ROWS, C), BF16),
            jax.ShapeDtypeStruct((8, C), F32),
        ),
        in_specs=[vmem] * 6 + [smem],
        out_specs=(vmem,) * 4,
        scratch_shapes=[
            pltpu.VMEM((FR + 2, RB + 2, W, C), BF16),
            pltpu.VMEM((FR + 2, RB + 2, W, C), BF16),
            pltpu.VMEM((FR + 2, RB + 2, W, C), BF16),
            pltpu.VMEM((FR + 2, 3 * C, RB * W), BF16),
            pltpu.VMEM((FR + 2, RB + 2, W, 3 * C), BF16),
            pltpu.VMEM((FR + 2, RB + 2, W, 3 * C), BF16),
            pltpu.VMEM((9, C, 3 * C), BF16),
            pltpu.VMEM((8, C), F32),
            pltpu.VMEM((PLANE, 8, C), F32),
            pltpu.VMEM((8, C), F32),
            pltpu.VMEM((LINE, 8, C), F32),
            pltpu.VMEM((8, C), F32),
            pltpu.VMEM((PLANE, 8, C), F32),
            pltpu.VMEM((16, C), F32),
            pltpu.VMEM((LINE, 16, C), F32),
            pltpu.VMEM((LINE, 8, C), F32),
            pltpu.VMEM((TAP_ROWS, C), BF16),
            pltpu.VMEM((HALF, C), BF16),
            pltpu.VMEM((REGION, C), BF16),
            pltpu.VMEM((PLANE, CHUNK, C), BF16),
            pltpu.VMEM((NZ, CHUNK, C), BF16),
            pltpu.VMEM((PLANE, CHUNK, C), BF16),
            pltpu.VMEM((PLANE, CHUNK, C), BF16),
            pltpu.VMEM((FR * RB * W, C), F32),
            pltpu.SemaphoreType.DMA((11,)),
            pltpu.SemaphoreType.DMA((11,)),
        ],
        compiler_params=pltpu.CompilerParams(
            collective_id=0, has_side_effects=True, vmem_limit_bytes=48 * 2**20
        ),
        cost_estimate=pl.CostEstimate(flops=3 * 10**9, bytes_accessed=4 * 10**6, transcendentals=10**6),
        name="block",
    )(
        frames,
        cotangent,
        conv_weight.reshape(9, 3 * C, C),
        conv_bias.reshape(1, C),
        norm_gain.reshape(1, C),
        norm_shift.reshape(1, C),
        clip_ids,
    )
    factor = 1.0 / math.sqrt(POSITIONS)
    weight_grad = wg.astype(F32).reshape(3, 3, 3, C, C) * factor
    return enc, fg, weight_grad, small[0], small[1], small[2]


def solution(mesh):
    placed = (P("span", None, "space", None, None),) * 2 + (P(),) * 5
    return jax.shard_map(
        local,
        mesh=mesh,
        in_specs=placed,
        out_specs=(P("span", None, "space", None, None),) * 2 + (P(),) * 4,
        check_vma=False,
    )
```

time: 563 us -> 61.7 us (0.11)
  waiting for transfers between devices: 259 us -> 0 us
  blocking collectives: 231 us -> 0 us
  Pallas kernels: 0 us -> 51.9 us
  between operations: 17.9 us -> 0.66 us
  matrix products: 17.2 us -> 0 us
  starting transfers between devices: 14.1 us -> 0 us
  other arithmetic: 11.2 us -> 1.32 us
    psum x1 -> x0, waiting for transfers between devices: 254 us -> none  [local(): lax.psum((weight_terms, bias_terms, gain_terms, shift_terms), ('span', 's...]
    psum x3 -> x0, blocking collectives: 231 us -> none  [the longest x1 81.4 us: local(): lax.psum(own_clip_hot[:, None] * local_sums[None, :], ('span', 'space'))]
    pallas_call x0 -> x1, Pallas kernels: none -> 51.9 us  [local(): pl.pallas_call(kernel, out_shape=(jax.ShapeDtypeStruct(frames.shape, BF16...]
    dot_general x27 -> x0, matrix products: 17.2 us -> none  [the longest x18 13.6 us: conv_block(): jnp.dot(window, kernel[time_tap, row_tap], preferred_element_type=jnp.flo...]
    ppermute x6 -> x0, starting transfers between devices: 14.1 us -> none  [the longest x2 6.23 us: padded_2(): before = lax.ppermute(last, axis, up)]
  transfers between devices with their start and end apart: 7 -> 0, of which waited for: 3 -> 0; matrix products, arithmetic and copies ran while one was open for 2% -> 0% of each run, Pallas kernels for 0% -> 0%
where the time goes in v1:
time: 61.7 us; the launch traced here: 61.4 us
  Pallas kernels  51.9 us (84%)
  local copies, waits for them, and re-layouts  7.6 us (12%)
  other arithmetic  1.32 us (2%)
  between operations  0.66 us (1%)
    pallas_call x1, Pallas kernels, local(): pl.pallas_call(kernel, out_shape=(jax.ShapeDtypeStruct(frames.shape, BF16...  51.9 us
    unnamed x16, local copies, waits for them, and re-layouts  7.08 us
    mul x1, other arithmetic, local(): weight_grad = wg.astype(F32).reshape(3, 3, 3, C, C) * factor  1.32 us

profile of v1, /device:TPU:1, one launch (start us, length us, event | category | flops | bytes accessed | tf_op | source)
XLA Modules:
  0.0 61.4 jit_solution(5408585661966316752)
XLA Ops:
  0.6 0.0 copy-start
  0.6 1.2 %copy-done = bf16[3,3,3,128,128]{4,3,2,1,0:T(8,128)(2,1)S(1)} copy-done((bf16[3,3,3,128,128]{4,3,2,1,0:T(8,128)(2,1)S(1)}, bf16[3,3,3,128,128]{4,3,2,1,0:T(8,128)(2,1)}, u32[]{:S(2)}) %copy-start) | copy-done | bytes 884760
  1.8 0.0 copy-start.1
  1.8 0.9 %copy-done.1 = bf16[1,4,2,128,128]{4,3,2,1,0:T(8,128)(2,1)S(1)} copy-done((bf16[1,4,2,128,128]{4,3,2,1,0:T(8,128)(2,1)S(1)}, bf16[1,4,2,128,128]{4,3,2,1,0:T(8,128)(2,1)}, u32[]{:S(2)}) %copy-start.1) | copy-done | bytes 262168
  2.8 0.0 copy-start.2
  2.8 0.9 %copy-done.2 = bf16[1,4,2,128,128]{4,3,2,1,0:T(8,128)(2,1)S(1)} copy-done((bf16[1,4,2,128,128]{4,3,2,1,0:T(8,128)(2,1)S(1)}, bf16[1,4,2,128,128]{4,3,2,1,0:T(8,128)(2,1)}, u32[]{:S(2)}) %copy-start.2) | copy-done | bytes 262168
  3.7 0.0 copy-start.3
  3.7 0.7 %copy-done.3 = f32[128]{0:T(128)S(1)} copy-done((f32[128]{0:T(128)S(1)}, f32[128]{0:T(128)}, u32[]{:S(2)}) %copy-start.3) | copy-done | bytes 536
  4.4 0.0 copy-start.4
  4.4 0.7 %copy-done.4 = f32[128]{0:T(128)S(1)} copy-done((f32[128]{0:T(128)S(1)}, f32[128]{0:T(128)}, u32[]{:S(2)}) %copy-start.4) | copy-done | bytes 536
  5.0 0.0 copy-start.5
  5.0 0.7 %copy-done.5 = f32[128]{0:T(128)S(1)} copy-done((f32[128]{0:T(128)S(1)}, f32[128]{0:T(128)}, u32[]{:S(2)}) %copy-start.5) | copy-done | bytes 536
  5.7 0.0 copy-start.6
  5.7 0.7 %copy-done.6 = s32[64]{0:T(128)S(1)} copy-done((s32[64]{0:T(128)S(1)}, s32[64]{0:T(128)}, u32[]{:S(2)}) %copy-start.6) | copy-done | bytes 280
  6.3 51.9 %block.1 = (bf16[1,4,2,128,128]{4,3,2,1,0:T(8,128)(2,1)S(1)}, bf16[1,4,2,128,128]{4,3,2,1,0:T(8,128)(2,1)S(1)}, bf16[3456,128]{1,0:T(8,128)(2,1)S(1)}, f32[8,128]{1,0:T(8,128)S(1)}) custom-call(bf16[1,4,2,128,128]{4,3,2,1,0:T(8,128)(2,1)S(1)} %copy-done.1, bf16[1,4,2,128,128]{4,3,2,1,0:T(8,128)(2,1)S(1)} %copy-done.2, bf16[9,384,128]{2,1,0:T(8,128)(2,1)S(1)} %bitcast.11, ...), custom_call_target="tpu_custom_call" | custom-call | flops 3000000000 | bytes 4000000 | tf_op jit(solution)/shard_map/block/pallas_call | solution.py:443
  58.2 0.5 slice_bitcast_fusion
  58.7 1.3 %convert_multiply_fusion = f32[3456,128]{1,0:T(8,128)} fusion(bf16[3456,128]{1,0:T(8,128)(2,1)S(1)} %get-tuple-element.12), kind=kLoop, calls=%fused_computation | loop fusion | flops 884736 | bytes 2654208 | tf_op jit(solution)/shard_map/mul | solution.py:496
  60.0 0.7 %copy.15 = bf16[1,4,2,128,128]{4,3,2,1,0:T(8,128)(2,1)} copy(bf16[1,4,2,128,128]{4,3,2,1,0:T(8,128)(2,1)S(1)} %get-tuple-element.23) | data formatting | bytes 524288
  60.7 0.7 %copy.16 = bf16[1,4,2,128,128]{4,3,2,1,0:T(8,128)(2,1)} copy(bf16[1,4,2,128,128]{4,3,2,1,0:T(8,128)(2,1)S(1)} %get-tuple-element.24) | data formatting | bytes 524288
Async XLA Ops:
  0.6 1.2 %copy-start = (bf16[3,3,3,128,128]{4,3,2,1,0:T(8,128)(2,1)S(1)}, bf16[3,3,3,128,128]{4,3,2,1,0:T(8,128)(2,1)}, u32[]{:S(2)}) copy-start(bf16[3,3,3,128,128]{4,3,2,1,0:T(8,128)(2,1)} %param.9) | copy-start | bytes 2654212
  1.8 0.9 %copy-start.1 = (bf16[1,4,2,128,128]{4,3,2,1,0:T(8,128)(2,1)S(1)}, bf16[1,4,2,128,128]{4,3,2,1,0:T(8,128)(2,1)}, u32[]{:S(2)}) copy-start(bf16[1,4,2,128,128]{4,3,2,1,0:T(8,128)(2,1)} %frames.1) | copy-start | bytes 786436
  2.8 0.9 %copy-start.2 = (bf16[1,4,2,128,128]{4,3,2,1,0:T(8,128)(2,1)S(1)}, bf16[1,4,2,128,128]{4,3,2,1,0:T(8,128)(2,1)}, u32[]{:S(2)}) copy-start(bf16[1,4,2,128,128]{4,3,2,1,0:T(8,128)(2,1)} %cot.1) | copy-start | bytes 786436
  3.7 0.7 %copy-start.3 = (f32[128]{0:T(128)S(1)}, f32[128]{0:T(128)}, u32[]{:S(2)}) copy-start(f32[128]{0:T(128)} %param.10) | copy-start | bytes 1540
  4.4 0.7 %copy-start.4 = (f32[128]{0:T(128)S(1)}, f32[128]{0:T(128)}, u32[]{:S(2)}) copy-start(f32[128]{0:T(128)} %param.11) | copy-start | bytes 1540
  5.0 0.7 %copy-start.5 = (f32[128]{0:T(128)S(1)}, f32[128]{0:T(128)}, u32[]{:S(2)}) copy-start(f32[128]{0:T(128)} %param.12) | copy-start | bytes 1540
  5.7 0.7 %copy-start.6 = (s32[64]{0:T(128)S(1)}, s32[64]{0:T(128)}, u32[]{:S(2)}) copy-start(s32[64]{0:T(128)} %clip.1) | copy-start | bytes 772

commit v2 on v1

--- a/solution.py
+++ b/solution.py
@@ -1,4 +1,3 @@
-import functools
 import math
 
 import jax
@@ -30,7 +29,12 @@
 CHUNK = 112
 REGION = PLANE * CHUNK
 
-(S_P1, S_P2, S_FH, S_CH, S_CORE, S_XY, S_Z, S_GXY, S_GCORE, S_Q1, S_Q2) = range(11)
+PARTS = (64, 48)
+STARTS = (0, PLANE * PARTS[0])
+
+(S_P1, S_P2, S_FH, S_CH, S_CORE, S_Q1, S_Q2) = range(7)
+S_XY, S_Z, S_GXY, S_GCORE = (7, 8), (9, 10), (11, 12), (13, 14)
+SEMS = 15
 
 
 def group_sum(v):
@@ -70,13 +74,32 @@
 
 
 def kernel(
-    frames, cot, wt, bias, gain, shift, clip,
+    frames_hbm, cot_hbm, wt_hbm, bias_hbm, gain_hbm, shift_hbm, clip_hbm,
     enc_out, fg_out, wg_out, small_out,
-    fp_buf, cp_buf, act, act_t, act_st, cot_st, wcat,
+    frames, cot, wt, bias, gain, shift, clip, fp_buf, cp_buf, act, act_t, act_st, cot_st, wcat,
     p1_src, p1, p2_src, p2, q1_src, q1, q2_src, q2, masks,
-    grads, r_core, s_xy, r_xy, r_z, t_xy, t_core, acc,
-    send, recv,
+    grads, r_core, s_xy, r_xy0, r_xy1, r_z0, r_z1, t_xy0, t_xy1, t_core0, t_core1, acc, out_acc,
+    send, recv, load,
 ):
+    arrays = (
+        (frames_hbm, frames), (clip_hbm, clip), (cot_hbm, cot), (gain_hbm, gain),
+        (shift_hbm, shift), (bias_hbm, bias), (wt_hbm, wt),
+    )
+    loads = [pltpu.make_async_copy(a, b, load.at[i]) for i, (a, b) in enumerate(arrays)]
+    loads[0].start()
+    r_xy, r_z, t_xy, t_core = (r_xy0, r_xy1), (r_z0, r_z1), (t_xy0, t_xy1), (t_core0, t_core1)
+    sent, arrived = [], set()
+
+    def receive(ref, which):
+        wait_for(ref, recv.at[which])
+        arrived.add(which)
+
+    def finish():
+        for ref, which in sent:
+            wait_for(ref, send.at[which])
+            if which not in arrived:
+                receive(ref, which)
+
     span = lax.axis_index("span")
     y = lax.axis_index("space")
     x = lax.div(span, LINE)
@@ -106,6 +129,11 @@
     for device in partners:
         pl.semaphore_signal(barrier, inc=1, device_id=device, device_id_type=MESH)
 
+    for copy in loads[1:]:
+        copy.start()
+
+    loads[0].wait()
+
     def add_rows(j, total):
         return total + rows_sum(frames[0, j // RB, j % RB].astype(F32))
 
@@ -125,11 +153,20 @@
     pl.semaphore_wait(barrier, len(partners))
     for o in PLANE_OFFS:
         push(p1_src, p1.at[plane], S_P1, in_plane(o))
+    sent.append((p1.at[pl.ds(0, PLANE - 1)], S_P1))
     push(frames.at[0, :, 1], fp_buf.at[pl.ds(2, FR), 0], S_FH, beside(0, 1))
     push(frames.at[0, :, 0], fp_buf.at[pl.ds(2, FR), 3], S_FH, beside(0, -1))
     push(frames.at[0, pl.ds(2, 2)], fp_buf.at[pl.ds(0, 2), pl.ds(1, RB)], S_FH, beside(1, 0))
     push(frames.at[0, pl.ds(2, 2), 1], fp_buf.at[pl.ds(0, 2), 0], S_FH, beside(1, 1))
     push(frames.at[0, pl.ds(2, 2), 0], fp_buf.at[pl.ds(0, 2), 3], S_FH, beside(1, -1))
+
+    sent.append((fp_buf.at[pl.ds(0, 4)], S_FH))
+    for copy in loads[1:]:
+        copy.wait()
+
+    for r in range(NC):
+        grads[r * REGION + HALF:(r + 1) * REGION] = jnp.zeros((REGION - HALF, C), F32)
+    r_core[HALF:REGION] = jnp.zeros((REGION - HALF, C), F32)
 
     own = clip[span]
     before = clip[lax.rem(span + SPANS - 1, SPANS)]
@@ -170,7 +207,7 @@
     bias_terms = lax.fori_loop(0, FR, stack_own, jnp.zeros((8, C), F32))
     bias_terms = jnp.sum(bias_terms, axis=0, keepdims=True)
 
-    wait_for(p1.at[pl.ds(0, PLANE - 1)], recv.at[S_P1])
+    receive(p1.at[pl.ds(0, PLANE - 1)], S_P1)
     mean_rows, square_rows = [], []
     for a in range(NX):
         parts = [p1[a * NY + b] for b in range(NY)]
@@ -184,12 +221,15 @@
     p2[line] = block
     for o in LINE_OFFS:
         push(p2_src, p2.at[line], S_P2, in_line(o))
+    sent.append((p2.at[pl.ds(0, LINE - 1)], S_P2))
     push(cot.at[0, :, 1], cp_buf.at[pl.ds(0, FR), 0], S_CH, beside(0, 1))
     push(cot.at[0, :, 0], cp_buf.at[pl.ds(0, FR), 3], S_CH, beside(0, -1))
     push(cot.at[0, pl.ds(0, 2)], cp_buf.at[pl.ds(4, 2), pl.ds(1, RB)], S_CH, beside(-1, 0))
     push(cot.at[0, pl.ds(0, 2), 1], cp_buf.at[pl.ds(4, 2), 0], S_CH, beside(-1, 1))
     push(cot.at[0, pl.ds(0, 2), 0], cp_buf.at[pl.ds(4, 2), 3], S_CH, beside(-1, -1))
 
+    sent.append((cp_buf.at[pl.ds(0, 4)], S_CH))
+
     def widen(t, carry):
         for ds in range(3):
             wcat[t, :, ds * C:(ds + 1) * C] = wt[t, pl.ds(ds * C, C)]
@@ -197,7 +237,7 @@
 
     lax.fori_loop(0, 9, widen, 0)
 
-    wait_for(fp_buf.at[pl.ds(0, 4)], recv.at[S_FH])
+    receive(fp_buf.at[pl.ds(0, 4)], S_FH)
 
     def carry_rows(r, carry):
         first = fp_buf[2, r].astype(F32) * starts
@@ -207,7 +247,7 @@
 
     lax.fori_loop(0, RB + 2, carry_rows, 0)
 
-    wait_for(p2.at[pl.ds(0, LINE - 1)], recv.at[S_P2])
+    receive(p2.at[pl.ds(0, LINE - 1)], S_P2)
     summed = jnp.zeros((8, C), F32)
     for k in range(LINE):
         summed = summed + p2[k] * masks[k]
@@ -241,37 +281,50 @@
 
     lax.fori_loop(0, FR + 2, activate, 0)
 
-    def tap_grad(t, carry):
+    cotangents = cot_st[0:FR, 1:1 + RB].reshape(FR * RB * W, 3 * C)
+    for k in range(3):
+        t = c * k + (1 - c) * (2 - k)
         left = jnp.concatenate([act_t[t + f] for f in range(FR)], axis=1)
-        right = cot_st[0:FR, 1:1 + RB].reshape(FR * RB * W, 3 * C)
-        g = jnp.dot(left, right, preferred_element_type=F32)
-        for dr in range(3):
-            for ds in range(3):
-                piece = g[dr * C:(dr + 1) * C, ds * C:(ds + 1) * C].astype(BF16)
-                grads[pl.ds(pl.multiple_of(t * 9 * C + (dr * 3 + ds) * C, C), C)] = piece
-        return carry
-
-    lax.fori_loop(0, 3, tap_grad, 0)
-    other = pl.multiple_of((1 - c) * HALF, 64)
-    push(grads.at[pl.ds(other, HALF)], r_core, S_CORE, in_line((0, 1)))
-    s_xy[HALF:REGION] = jnp.zeros((REGION - HALF, C), BF16)
-    wait_for(r_core, recv.at[S_CORE])
-    mine = pl.multiple_of(c * HALF, 64)
-
-    def add_core(k, carry):
-        at = pl.multiple_of(k * 64, 64)
-        own_part = grads[pl.ds(pl.multiple_of(mine + at, 64), 64)].astype(F32)
-        s_xy[pl.ds(at, 64)] = (own_part + r_core[pl.ds(at, 64)].astype(F32)).astype(BF16)
-        return carry
-
-    lax.fori_loop(0, HALF // 64, add_core, 0)
-    for o in PLANE_OFFS:
-        px, py = lax.rem(x + o[0], NX), lax.rem(y + o[1], NY)
-        at = pl.multiple_of((px * NY + py) * CHUNK, 16)
-        push(s_xy.at[pl.ds(at, CHUNK)], r_xy.at[plane], S_XY, in_plane(o))
-    r_xy[plane] = s_xy[pl.ds(pl.multiple_of(plane * CHUNK, 16), CHUNK)]
-
-    wait_for(cp_buf.at[pl.ds(0, 4)], recv.at[S_CH])
+        g = jnp.dot(left, cotangents, preferred_element_type=F32)
+        for b in range(9):
+            dr, ds = b // 3, b % 3
+            piece = g[dr * C:(dr + 1) * C, ds * C:(ds + 1) * C]
+            if k != 1:
+                at = pl.multiple_of(t * (9 * C + 32) + b * C, 64)
+                grads[pl.ds(at, C)] = piece
+            elif b != 4:
+                at = (9 + b) * C + (REGION - HALF if b > 4 else 0)
+                grads[at:at + C] = piece
+            else:
+                grads[HALF - 64:HALF] = piece[0:64]
+                grads[REGION:REGION + 64] = piece[64:128]
+        if k < 2:
+            size = (9 * C, HALF - 9 * C)[k]
+            source = ((1 - c) * 2 * (9 * C + 32), c * 9 * C + (1 - c) * REGION)[k]
+            target = ((1 - c) * (HALF - 9 * C), c * 9 * C)[k]
+            push(
+                grads.at[pl.ds(pl.multiple_of(source, 64), size)],
+                r_core.at[pl.ds(pl.multiple_of(target, 64), size)],
+                S_CORE, in_line((0, 1)),
+            )
+    sent.append((r_core.at[pl.ds(0, HALF)], S_CORE))
+    receive(r_core.at[pl.ds(0, HALF)], S_CORE)
+    mine = c * REGION
+
+    def both_cores(at, rows):
+        a = grads[pl.ds(pl.multiple_of(mine + at, 16), rows)]
+        return (a + r_core[pl.ds(pl.multiple_of(at, 16), rows)]).astype(BF16)
+
+    for h, rows in enumerate(PARTS):
+        for o in PLANE_OFFS:
+            px, py = lax.rem(x + o[0], NX), lax.rem(y + o[1], NY)
+            at = pl.multiple_of(STARTS[h] + (px * NY + py) * rows, 16)
+            s_xy[pl.ds(at, rows)] = both_cores(at, rows)
+            push(s_xy.at[pl.ds(at, rows)], r_xy[h].at[plane], S_XY[h], in_plane(o))
+        sent.append((r_xy[h].at[pl.ds(0, PLANE - 1)], S_XY[h]))
+        r_xy[h][plane] = both_cores(STARTS[h] + plane * rows, rows)
+
+    receive(cp_buf.at[pl.ds(0, 4)], S_CH)
 
     def stack_sides(f, carry):
         stack_cot(cp_buf[f, 0].astype(F32) * above, f, 0)
@@ -331,13 +384,20 @@
     for o in PLANE_OFFS:
         push(q1_src, q1.at[plane], S_Q1, in_plane(o))
 
-    wait_for(r_xy.at[pl.ds(0, PLANE - 1)], recv.at[S_XY])
-    total = r_xy[0].astype(F32)
-    for k in range(1, PLANE):
-        total = total + r_xy[k].astype(F32)
-    r_z[z] = total.astype(BF16)
-    for o in Z_OFFS:
-        push(r_z.at[z], r_z.at[z], S_Z, in_line((o, 0)))
+    sent.append((q1.at[pl.ds(0, PLANE - 1)], S_Q1))
+
+    def add_up(ref, count):
+        total = ref[0].astype(F32)
+        for k in range(1, count):
+            total = total + ref[k].astype(F32)
+        return total.astype(BF16)
+
+    for h in range(2):
+        receive(r_xy[h].at[pl.ds(0, PLANE - 1)], S_XY[h])
+        r_z[h][z] = add_up(r_xy[h], PLANE)
+        for o in Z_OFFS:
+            push(r_z[h].at[z], r_z[h].at[z], S_Z[h], in_line((o, 0)))
+        sent.append((r_z[h].at[pl.ds(0, NZ - 1)], S_Z[h]))
 
     def stack_act(f, carry):
         for r in range(RB + 2):
@@ -348,8 +408,25 @@
         return carry
 
     lax.fori_loop(0, FR + 2, stack_act, 0)
-
-    wait_for(q1.at[pl.ds(0, PLANE - 1)], recv.at[S_Q1])
+    out_acc[...] = jnp.zeros_like(out_acc) + bias[...]
+
+    def forward_tap(t, carry):
+        dt, dr = lax.div(t, 3), lax.rem(t, 3)
+        window = act_st[pl.ds(dt, FR), pl.ds(dr, RB)].reshape(FR * RB * W, 3 * C)
+        out_acc[...] += jnp.dot(window, wt[t], preferred_element_type=F32)
+        return carry
+
+    lax.fori_loop(0, 9, forward_tap, 0)
+    enc_out[0] = out_acc[...].astype(BF16).reshape(FR, RB, W, C)
+
+    for h in range(2):
+        receive(r_z[h].at[pl.ds(0, NZ - 1)], S_Z[h])
+        t_xy[h][plane] = add_up(r_z[h], NZ)
+        for o in PLANE_OFFS:
+            push(t_xy[h].at[plane], t_xy[h].at[plane], S_GXY[h], in_plane(o))
+        sent.append((t_xy[h].at[pl.ds(0, PLANE - 1)], S_GXY[h]))
+
+    receive(q1.at[pl.ds(0, PLANE - 1)], S_Q1)
     rows = []
     bias_sum = jnp.zeros((1, C), F32)
     for a in range(NX):
@@ -363,17 +440,21 @@
     q2[line] = block
     for o in LINE_OFFS:
         push(q2_src, q2.at[line], S_Q2, in_line(o))
-
-    wait_for(r_z.at[pl.ds(0, NZ - 1)], recv.at[S_Z])
-    total = r_z[0].astype(F32)
-    for k in range(1, NZ):
-        total = total + r_z[k].astype(F32)
-    t_xy[plane] = total.astype(BF16)
-    for o in PLANE_OFFS:
-        push(t_xy.at[plane], t_xy.at[plane], S_GXY, in_plane(o))
-
-
-    wait_for(q2.at[pl.ds(0, LINE - 1)], recv.at[S_Q2])
+    sent.append((q2.at[pl.ds(0, LINE - 1)], S_Q2))
+
+    def write(ref, h, region):
+        size = min(PLANE * PARTS[h], HALF - STARTS[h])
+        at = pl.multiple_of(region * HALF + STARTS[h], 64)
+        wg_out[pl.ds(at, size)] = ref[h][...].reshape(PLANE * PARTS[h], C)[0:size]
+
+    def hand_over(h):
+        receive(t_xy[h].at[pl.ds(0, PLANE - 1)], S_GXY[h])
+        push(t_xy[h], t_core[h], S_GCORE[h], in_line((0, 1)))
+        sent.append((t_core[h], S_GCORE[h]))
+
+    hand_over(0)
+
+    receive(q2.at[pl.ds(0, LINE - 1)], S_Q2)
     summed = jnp.zeros((8, C), F32)
     whole = jnp.zeros((16, C), F32)
     for k in range(LINE):
@@ -402,44 +483,50 @@
 
     lax.fori_loop(0, FR * RB, frame_grads, 0)
 
-    acc[...] = jnp.zeros_like(acc) + bias[...]
-
-    def forward_tap(t, carry):
-        dt, dr = lax.div(t, 3), lax.rem(t, 3)
-        window = act_st[pl.ds(dt, FR), pl.ds(dr, RB)].reshape(FR * RB * W, 3 * C)
-        acc[...] += jnp.dot(window, wt[t], preferred_element_type=F32)
-        return carry
-
-    lax.fori_loop(0, 9, forward_tap, 0)
-    enc_out[0] = acc[...].astype(BF16).reshape(FR, RB, W, C)
-
-    wait_for(t_xy.at[pl.ds(0, PLANE - 1)], recv.at[S_GXY])
-    push(t_xy, t_core, S_GCORE, in_line((0, 1)))
-
-    def write(src, base):
-        at = pl.multiple_of(base, 64)
-        wg_out[pl.ds(at, HALF)] = src[...].reshape(REGION, C)[0:HALF]
-
-    write(t_xy, c * HALF)
-    wait_for(t_core, recv.at[S_GCORE])
-    write(t_core, (1 - c) * HALF)
-
-    wait_for(p1.at[pl.ds(0, PLANE - 1)], send.at[S_P1])
-    wait_for(p2.at[pl.ds(0, LINE - 1)], send.at[S_P2])
-    wait_for(fp_buf.at[pl.ds(0, 4)], send.at[S_FH])
-    wait_for(cp_buf.at[pl.ds(0, 4)], send.at[S_CH])
-    wait_for(r_core, send.at[S_CORE])
-    wait_for(r_xy.at[pl.ds(0, PLANE - 1)], send.at[S_XY])
-    wait_for(r_z.at[pl.ds(0, NZ - 1)], send.at[S_Z])
-    wait_for(t_xy.at[pl.ds(0, PLANE - 1)], send.at[S_GXY])
-    wait_for(t_core, send.at[S_GCORE])
-    wait_for(q1.at[pl.ds(0, PLANE - 1)], send.at[S_Q1])
-    wait_for(q2.at[pl.ds(0, LINE - 1)], send.at[S_Q2])
+    hand_over(1)
+    write(t_xy, 0, c)
+    write(t_xy, 1, c)
+    for h in range(2):
+        receive(t_core[h], S_GCORE[h])
+        write(t_core, h, 1 - c)
+    finish()
+
+
+def writer(enc, fg, wg, small, enc_out, fg_out, wg_out, bias_out, gain_out, shift_out, wide, sems):
+    copies = [
+        pltpu.make_async_copy(enc, enc_out, sems.at[0]),
+        pltpu.make_async_copy(fg, fg_out, sems.at[1]),
+    ]
+    for copy in copies:
+        copy.start()
+    factor = 1.0 / math.sqrt(POSITIONS)
+    part = TAP_ROWS // 3
+    for k in range(3):
+        at = pl.ds(k * part, part)
+        wide[at] = wg[at].astype(F32) * factor
+        copy = pltpu.make_async_copy(wide.at[at], wg_out.at[at], sems.at[2 + k])
+        copy.start()
+        copies.append(copy)
+    bias_out[...] = small[0:1]
+    gain_out[...] = small[1:2]
+    shift_out[...] = small[2:3]
+    for copy in copies:
+        copy.wait()
 
 
 def local(frames, cotangent, conv_weight, conv_bias, norm_gain, norm_shift, clip_ids):
     vmem = pl.BlockSpec(memory_space=pltpu.VMEM)
-    smem = pl.BlockSpec(memory_space=pltpu.SMEM)
+    hbm = pl.BlockSpec(memory_space=pltpu.HBM)
+    row = jax.ShapeDtypeStruct((1, C), F32)
+    operands = (
+        frames,
+        cotangent,
+        conv_weight.reshape(9, 3 * C, C),
+        conv_bias.reshape(1, C),
+        norm_gain.reshape(1, C),
+        norm_shift.reshape(1, C),
+        clip_ids,
+    )
     enc, fg, wg, small = pl.pallas_call(
         kernel,
         out_shape=(
@@ -448,9 +535,16 @@
             jax.ShapeDtypeStruct((TAP_ROWS, C), BF16),
             jax.ShapeDtypeStruct((8, C), F32),
         ),
-        in_specs=[vmem] * 6 + [smem],
+        in_specs=[hbm] * 7,
         out_specs=(vmem,) * 4,
         scratch_shapes=[
+            pltpu.VMEM(frames.shape, BF16),
+            pltpu.VMEM(frames.shape, BF16),
+            pltpu.VMEM((9, 3 * C, C), BF16),
+            pltpu.VMEM((1, C), F32),
+            pltpu.VMEM((1, C), F32),
+            pltpu.VMEM((1, C), F32),
+            pltpu.SMEM((SPANS,), jnp.int32),
             pltpu.VMEM((FR + 2, RB + 2, W, C), BF16),
             pltpu.VMEM((FR + 2, RB + 2, W, C), BF16),
             pltpu.VMEM((FR + 2, RB + 2, W, C), BF16),
@@ -467,34 +561,43 @@
             pltpu.VMEM((16, C), F32),
             pltpu.VMEM((LINE, 16, C), F32),
             pltpu.VMEM((LINE, 8, C), F32),
-            pltpu.VMEM((TAP_ROWS, C), BF16),
-            pltpu.VMEM((HALF, C), BF16),
+            pltpu.VMEM((NC * REGION, C), F32),
+            pltpu.VMEM((REGION, C), F32),
             pltpu.VMEM((REGION, C), BF16),
-            pltpu.VMEM((PLANE, CHUNK, C), BF16),
-            pltpu.VMEM((NZ, CHUNK, C), BF16),
-            pltpu.VMEM((PLANE, CHUNK, C), BF16),
-            pltpu.VMEM((PLANE, CHUNK, C), BF16),
+            *[pltpu.VMEM((PLANE, rows, C), BF16) for rows in PARTS],
+            *[pltpu.VMEM((NZ, rows, C), BF16) for rows in PARTS],
+            *[pltpu.VMEM((PLANE, rows, C), BF16) for rows in PARTS],
+            *[pltpu.VMEM((PLANE, rows, C), BF16) for rows in PARTS],
             pltpu.VMEM((FR * RB * W, C), F32),
-            pltpu.SemaphoreType.DMA((11,)),
-            pltpu.SemaphoreType.DMA((11,)),
+            pltpu.VMEM((FR * RB * W, C), F32),
+            pltpu.SemaphoreType.DMA((SEMS,)),
+            pltpu.SemaphoreType.DMA((SEMS,)),
+            pltpu.SemaphoreType.DMA((7,)),
         ],
         compiler_params=pltpu.CompilerParams(
             collective_id=0, has_side_effects=True, vmem_limit_bytes=48 * 2**20
         ),
         cost_estimate=pl.CostEstimate(flops=3 * 10**9, bytes_accessed=4 * 10**6, transcendentals=10**6),
         name="block",
-    )(
-        frames,
-        cotangent,
-        conv_weight.reshape(9, 3 * C, C),
-        conv_bias.reshape(1, C),
-        norm_gain.reshape(1, C),
-        norm_shift.reshape(1, C),
-        clip_ids,
+    )(*(pltpu.with_memory_space_constraint(v, pltpu.HBM) for v in operands))
+    enc, fg, wg, bias, gain, shift = pl.pallas_call(
+        writer,
+        out_shape=(
+            jax.ShapeDtypeStruct(frames.shape, BF16),
+            jax.ShapeDtypeStruct(frames.shape, BF16),
+            jax.ShapeDtypeStruct((TAP_ROWS, C), F32),
+            row, row, row,
+        ),
+        in_specs=[vmem] * 4,
+        out_specs=(hbm,) * 3 + (vmem,) * 3,
+        scratch_shapes=[pltpu.VMEM((TAP_ROWS, C), F32), pltpu.SemaphoreType.DMA((5,))],
+        compiler_params=pltpu.CompilerParams(vmem_limit_bytes=32 * 2**20),
+        name="writer",
+    )(enc, fg, wg, small)
+    return (
+        enc, fg, wg.reshape(conv_weight.shape),
+        bias.reshape(C), gain.reshape(C), shift.reshape(C),
     )
-    factor = 1.0 / math.sqrt(POSITIONS)
-    weight_grad = wg.astype(F32).reshape(3, 3, 3, C, C) * factor
-    return enc, fg, weight_grad, small[0], small[1], small[2]
 
 
 def solution(mesh):

time: 61.7 us -> 50.4 us (0.82)
  local copies, waits for them, and re-layouts: 7.6 us -> 0 us
  Pallas kernels: 51.9 us -> 49.6 us
  other arithmetic: 1.32 us -> 0 us
    unnamed x16 -> x0, local copies, waits for them, and re-layouts: 7.08 us -> none
    pallas_call x1, Pallas kernels: 51.9 us -> 47.7 us  [local(): pl.pallas_call(kernel, out_shape=(jax.ShapeDtypeStruct(frames.shape, BF16...]
    pallas_call x0 -> x1, Pallas kernels: none -> 1.94 us  [local(): pl.pallas_call(writer, out_shape=(jax.ShapeDtypeStruct(frames.shape, BF16...]
    mul x1 -> x0, other arithmetic: 1.32 us -> none  [local(): weight_grad = wg.astype(F32).reshape(3, 3, 3, C, C) * factor]
where the time goes in v2:
time: 50.4 us; the launch traced here: 50.3 us
  Pallas kernels  49.6 us (98%)
  between operations  0.64 us (1%)
    pallas_call x1, Pallas kernels, local(): pl.pallas_call(kernel, out_shape=(jax.ShapeDtypeStruct(frames.shape, BF16...  47.7 us
    pallas_call x1, Pallas kernels, local(): pl.pallas_call(writer, out_shape=(jax.ShapeDtypeStruct(frames.shape, BF16...  1.94 us

profile of v2, /device:TPU:1, one launch (start us, length us, event | category | flops | bytes accessed | tf_op | source)
XLA Modules:
  0.0 50.3 jit_solution(1161418230590952351)
XLA Ops:
  0.6 47.7 %block.1 = (bf16[1,4,2,128,128]{4,3,2,1,0:T(8,128)(2,1)S(1)}, bf16[1,4,2,128,128]{4,3,2,1,0:T(8,128)(2,1)S(1)}, bf16[3456,128]{1,0:T(8,128)(2,1)S(1)}, f32[8,128]{1,0:T(8,128)S(1)}) custom-call(bf16[1,4,2,128,128]{4,3,2,1,0:T(8,128)(2,1)} %frames_hbm.1, bf16[1,4,2,128,128]{4,3,2,1,0:T(8,128)(2,1)} %cot_hbm.1, bf16[9,384,128]{2,1,0:T(8,128)(2,1)} %bitcast.9, ...), custom_call_target="tpu_custom_call" | custom-call | flops 3000000000 | bytes 4000000 | tf_op jit(solution)/shard_map/block/pallas_call | solution.py:530
  48.3 1.9 %writer.1 = (bf16[1,4,2,128,128]{4,3,2,1,0:T(8,128)(2,1)}, bf16[1,4,2,128,128]{4,3,2,1,0:T(8,128)(2,1)}, f32[3456,128]{1,0:T(8,128)}, f32[1,128]{1,0:T(1,128)}, f32[1,128]{1,0:T(1,128)}, /*index=5*/f32[1,128]{1,0:T(1,128)}) custom-call(bf16[1,4,2,128,128]{4,3,2,1,0:T(8,128)(2,1)S(1)} %get-tuple-element.16.enc, ...), custom_call_target="tpu_custom_call" | custom-call | tf_op jit(solution)/shard_map/writer/pallas_call | solution.py:583

commit v3 on v2

--- a/solution.py
+++ b/solution.py
@@ -26,14 +26,12 @@
 PER_SPAN = PER_DEVICE * NY
 TAP_ROWS = 27 * C
 HALF = TAP_ROWS // 2
-CHUNK = 112
-REGION = PLANE * CHUNK
-
-PARTS = (64, 48)
-STARTS = (0, PLANE * PARTS[0])
+CHUNK_P, CHUNK_Q = 80, 64
+ROWS_P, ROWS_Q = PLANE * CHUNK_P, NZ * CHUNK_Q
+REGION = ROWS_P + ROWS_Q
 
 (S_P1, S_P2, S_FH, S_CH, S_CORE, S_Q1, S_Q2) = range(7)
-S_XY, S_Z, S_GXY, S_GCORE = (7, 8), (9, 10), (11, 12), (13, 14)
+(S_PA, S_PB, S_PC, S_PD, S_QA, S_QB, S_QC, S_QD) = range(7, 15)
 SEMS = 15
 
 
@@ -78,7 +76,7 @@
     enc_out, fg_out, wg_out, small_out,
     frames, cot, wt, bias, gain, shift, clip, fp_buf, cp_buf, act, act_t, act_st, cot_st, wcat,
     p1_src, p1, p2_src, p2, q1_src, q1, q2_src, q2, masks,
-    grads, r_core, s_xy, r_xy0, r_xy1, r_z0, r_z1, t_xy0, t_xy1, t_core0, t_core1, acc, out_acc,
+    grads, r_core, s_xy, pa, pb, pc, pd, qa, qb, qc, qd, acc, out_acc,
     send, recv, load,
 ):
     arrays = (
@@ -87,7 +85,6 @@
     )
     loads = [pltpu.make_async_copy(a, b, load.at[i]) for i, (a, b) in enumerate(arrays)]
     loads[0].start()
-    r_xy, r_z, t_xy, t_core = (r_xy0, r_xy1), (r_z0, r_z1), (t_xy0, t_xy1), (t_core0, t_core1)
     sent, arrived = [], set()
 
     def receive(ref, which):
@@ -126,6 +123,9 @@
     barrier = pltpu.get_barrier_semaphore()
     partners = [in_plane(o) for o in PLANE_OFFS] + [in_line(o) for o in LINE_OFFS]
     partners += [beside(ds, dy) for ds in (-1, 1) for dy in (-1, 0, 1)]
+    far = [distance(a, NX) + distance(b, NY) for a, b in PLANE_OFFS]
+    far += [distance(a, NZ) + b for a, b in LINE_OFFS] + [2.5, 1.5, 2.5] * 2
+    partners = [device for _, device in sorted(zip(far, partners), key=lambda p: -p[0])]
     for device in partners:
         pl.semaphore_signal(barrier, inc=1, device_id=device, device_id_type=MESH)
 
@@ -315,14 +315,19 @@
         a = grads[pl.ds(pl.multiple_of(mine + at, 16), rows)]
         return (a + r_core[pl.ds(pl.multiple_of(at, 16), rows)]).astype(BF16)
 
-    for h, rows in enumerate(PARTS):
-        for o in PLANE_OFFS:
-            px, py = lax.rem(x + o[0], NX), lax.rem(y + o[1], NY)
-            at = pl.multiple_of(STARTS[h] + (px * NY + py) * rows, 16)
-            s_xy[pl.ds(at, rows)] = both_cores(at, rows)
-            push(s_xy.at[pl.ds(at, rows)], r_xy[h].at[plane], S_XY[h], in_plane(o))
-        sent.append((r_xy[h].at[pl.ds(0, PLANE - 1)], S_XY[h]))
-        r_xy[h][plane] = both_cores(STARTS[h] + plane * rows, rows)
+    for o in PLANE_OFFS:
+        px, py = lax.rem(x + o[0], NX), lax.rem(y + o[1], NY)
+        at = pl.multiple_of((px * NY + py) * CHUNK_P, 16)
+        s_xy[pl.ds(at, CHUNK_P)] = both_cores(at, CHUNK_P)
+        push(s_xy.at[pl.ds(at, CHUNK_P)], pa.at[plane], S_PA, in_plane(o))
+    for o in Z_OFFS:
+        at = pl.multiple_of(ROWS_P + lax.rem(z + o, NZ) * CHUNK_Q, 16)
+        s_xy[pl.ds(at, CHUNK_Q)] = both_cores(at, CHUNK_Q)
+        push(s_xy.at[pl.ds(at, CHUNK_Q)], qa.at[z], S_QA, in_line((o, 0)))
+    sent.append((pa.at[pl.ds(0, PLANE - 1)], S_PA))
+    sent.append((qa.at[pl.ds(0, NZ - 1)], S_QA))
+    pa[plane] = both_cores(plane * CHUNK_P, CHUNK_P)
+    qa[z] = both_cores(ROWS_P + z * CHUNK_Q, CHUNK_Q)
 
     receive(cp_buf.at[pl.ds(0, 4)], S_CH)
 
@@ -386,19 +391,6 @@
 
     sent.append((q1.at[pl.ds(0, PLANE - 1)], S_Q1))
 
-    def add_up(ref, count):
-        total = ref[0].astype(F32)
-        for k in range(1, count):
-            total = total + ref[k].astype(F32)
-        return total.astype(BF16)
-
-    for h in range(2):
-        receive(r_xy[h].at[pl.ds(0, PLANE - 1)], S_XY[h])
-        r_z[h][z] = add_up(r_xy[h], PLANE)
-        for o in Z_OFFS:
-            push(r_z[h].at[z], r_z[h].at[z], S_Z[h], in_line((o, 0)))
-        sent.append((r_z[h].at[pl.ds(0, NZ - 1)], S_Z[h]))
-
     def stack_act(f, carry):
         for r in range(RB + 2):
             v = act[f, r].astype(F32)
@@ -408,6 +400,24 @@
         return carry
 
     lax.fori_loop(0, FR + 2, stack_act, 0)
+
+    def add_up(ref, count):
+        total = ref[0].astype(F32)
+        for k in range(1, count):
+            total = total + ref[k].astype(F32)
+        return total.astype(BF16)
+
+    receive(qa.at[pl.ds(0, NZ - 1)], S_QA)
+    qb[plane] = add_up(qa, NZ)
+    for o in PLANE_OFFS:
+        push(qb.at[plane], qb.at[plane], S_QB, in_plane(o))
+    sent.append((qb.at[pl.ds(0, PLANE - 1)], S_QB))
+    receive(pa.at[pl.ds(0, PLANE - 1)], S_PA)
+    pb[z] = add_up(pa, PLANE)
+    for o in Z_OFFS:
+        push(pb.at[z], pb.at[z], S_PB, in_line((o, 0)))
+    sent.append((pb.at[pl.ds(0, NZ - 1)], S_PB))
+
     out_acc[...] = jnp.zeros_like(out_acc) + bias[...]
 
     def forward_tap(t, carry):
@@ -416,15 +426,7 @@
         out_acc[...] += jnp.dot(window, wt[t], preferred_element_type=F32)
         return carry
 
-    lax.fori_loop(0, 9, forward_tap, 0)
-    enc_out[0] = out_acc[...].astype(BF16).reshape(FR, RB, W, C)
-
-    for h in range(2):
-        receive(r_z[h].at[pl.ds(0, NZ - 1)], S_Z[h])
-        t_xy[h][plane] = add_up(r_z[h], NZ)
-        for o in PLANE_OFFS:
-            push(t_xy[h].at[plane], t_xy[h].at[plane], S_GXY[h], in_plane(o))
-        sent.append((t_xy[h].at[pl.ds(0, PLANE - 1)], S_GXY[h]))
+    lax.fori_loop(0, 5, forward_tap, 0)
 
     receive(q1.at[pl.ds(0, PLANE - 1)], S_Q1)
     rows = []
@@ -441,18 +443,27 @@
     for o in LINE_OFFS:
         push(q2_src, q2.at[line], S_Q2, in_line(o))
     sent.append((q2.at[pl.ds(0, LINE - 1)], S_Q2))
-
-    def write(ref, h, region):
-        size = min(PLANE * PARTS[h], HALF - STARTS[h])
-        at = pl.multiple_of(region * HALF + STARTS[h], 64)
-        wg_out[pl.ds(at, size)] = ref[h][...].reshape(PLANE * PARTS[h], C)[0:size]
-
-    def hand_over(h):
-        receive(t_xy[h].at[pl.ds(0, PLANE - 1)], S_GXY[h])
-        push(t_xy[h], t_core[h], S_GCORE[h], in_line((0, 1)))
-        sent.append((t_core[h], S_GCORE[h]))
-
-    hand_over(0)
+    lax.fori_loop(5, 9, forward_tap, 0)
+    enc_out[0] = out_acc[...].astype(BF16).reshape(FR, RB, W, C)
+
+    receive(pb.at[pl.ds(0, NZ - 1)], S_PB)
+    pc[plane] = add_up(pb, NZ)
+    for o in PLANE_OFFS:
+        push(pc.at[plane], pc.at[plane], S_PC, in_plane(o))
+    sent.append((pc.at[pl.ds(0, PLANE - 1)], S_PC))
+    receive(qb.at[pl.ds(0, PLANE - 1)], S_QB)
+    qc[z] = add_up(qb, PLANE)
+    for o in Z_OFFS:
+        push(qc.at[z], qc.at[z], S_QC, in_line((o, 0)))
+    sent.append((qc.at[pl.ds(0, NZ - 1)], S_QC))
+
+
+    def write(ref_p, ref_q, region):
+        at = pl.multiple_of(region * HALF, 64)
+        wg_out[pl.ds(at, ROWS_P)] = ref_p[...].reshape(ROWS_P, C)
+        at = pl.multiple_of(region * HALF + ROWS_P, 64)
+        wg_out[pl.ds(at, HALF - ROWS_P)] = ref_q[...].reshape(ROWS_Q, C)[0:HALF - ROWS_P]
+
 
     receive(q2.at[pl.ds(0, LINE - 1)], S_Q2)
     summed = jnp.zeros((8, C), F32)
@@ -483,12 +494,16 @@
 
     lax.fori_loop(0, FR * RB, frame_grads, 0)
 
-    hand_over(1)
-    write(t_xy, 0, c)
-    write(t_xy, 1, c)
-    for h in range(2):
-        receive(t_core[h], S_GCORE[h])
-        write(t_core, h, 1 - c)
+    receive(qc.at[pl.ds(0, NZ - 1)], S_QC)
+    push(qc, qd, S_QD, in_line((0, 1)))
+    sent.append((qd, S_QD))
+    receive(pc.at[pl.ds(0, PLANE - 1)], S_PC)
+    push(pc, pd, S_PD, in_line((0, 1)))
+    sent.append((pd, S_PD))
+    write(pc, qc, c)
+    receive(qd, S_QD)
+    receive(pd, S_PD)
+    write(pd, qd, 1 - c)
     finish()
 
 
@@ -564,10 +579,14 @@
             pltpu.VMEM((NC * REGION, C), F32),
             pltpu.VMEM((REGION, C), F32),
             pltpu.VMEM((REGION, C), BF16),
-            *[pltpu.VMEM((PLANE, rows, C), BF16) for rows in PARTS],
-            *[pltpu.VMEM((NZ, rows, C), BF16) for rows in PARTS],
-            *[pltpu.VMEM((PLANE, rows, C), BF16) for rows in PARTS],
-            *[pltpu.VMEM((PLANE, rows, C), BF16) for rows in PARTS],
+            pltpu.VMEM((PLANE, CHUNK_P, C), BF16),
+            pltpu.VMEM((NZ, CHUNK_P, C), BF16),
+            pltpu.VMEM((PLANE, CHUNK_P, C), BF16),
+            pltpu.VMEM((PLANE, CHUNK_P, C), BF16),
+            pltpu.VMEM((NZ, CHUNK_Q, C), BF16),
+            pltpu.VMEM((PLANE, CHUNK_Q, C), BF16),
+            pltpu.VMEM((NZ, CHUNK_Q, C), BF16),
+            pltpu.VMEM((NZ, CHUNK_Q, C), BF16),
             pltpu.VMEM((FR * RB * W, C), F32),
             pltpu.VMEM((FR * RB * W, C), F32),
             pltpu.SemaphoreType.DMA((SEMS,)),

time: 50.4 us -> 49.7 us (0.986)
  Pallas kernels: 49.6 us -> 48.9 us
    pallas_call x1, Pallas kernels: 47.7 us -> 47 us  [local(): pl.pallas_call(kernel, out_shape=(jax.ShapeDtypeStruct(frames.shape, BF16...]
where the time goes in v3:
time: 49.7 us; the launch traced here: 49.6 us
  Pallas kernels  48.9 us (98%)
  between operations  0.64 us (1%)
    pallas_call x1, Pallas kernels, local(): pl.pallas_call(kernel, out_shape=(jax.ShapeDtypeStruct(frames.shape, BF16...  47 us
    pallas_call x1, Pallas kernels, local(): pl.pallas_call(writer, out_shape=(jax.ShapeDtypeStruct(frames.shape, BF16...  1.94 us

profile of v3, /device:TPU:1, one launch (start us, length us, event | category | flops | bytes accessed | tf_op | source)
XLA Modules:
  0.0 49.6 jit_solution(18253193680524239883)
XLA Ops:
  0.6 47.0 %block.1 = (bf16[1,4,2,128,128]{4,3,2,1,0:T(8,128)(2,1)S(1)}, bf16[1,4,2,128,128]{4,3,2,1,0:T(8,128)(2,1)S(1)}, bf16[3456,128]{1,0:T(8,128)(2,1)S(1)}, f32[8,128]{1,0:T(8,128)S(1)}) custom-call(bf16[1,4,2,128,128]{4,3,2,1,0:T(8,128)(2,1)} %frames_hbm.1, bf16[1,4,2,128,128]{4,3,2,1,0:T(8,128)(2,1)} %cot_hbm.1, bf16[9,384,128]{2,1,0:T(8,128)(2,1)} %bitcast.9, ...), custom_call_target="tpu_custom_call" | custom-call | flops 3000000000 | bytes 4000000 | tf_op jit(solution)/shard_map/block/pallas_call | solution.py:545
  47.6 1.9 %writer.1 = (bf16[1,4,2,128,128]{4,3,2,1,0:T(8,128)(2,1)}, bf16[1,4,2,128,128]{4,3,2,1,0:T(8,128)(2,1)}, f32[3456,128]{1,0:T(8,128)}, f32[1,128]{1,0:T(1,128)}, f32[1,128]{1,0:T(1,128)}, /*index=5*/f32[1,128]{1,0:T(1,128)}) custom-call(bf16[1,4,2,128,128]{4,3,2,1,0:T(8,128)(2,1)S(1)} %get-tuple-element.16.enc, ...), custom_call_target="tpu_custom_call" | custom-call | tf_op jit(solution)/shard_map/writer/pallas_call | solution.py:602

commit v4 on v3

--- a/solution.py
+++ b/solution.py
@@ -76,7 +76,7 @@
     enc_out, fg_out, wg_out, small_out,
     frames, cot, wt, bias, gain, shift, clip, fp_buf, cp_buf, act, act_t, act_st, cot_st, wcat,
     p1_src, p1, p2_src, p2, q1_src, q1, q2_src, q2, masks,
-    grads, r_core, s_xy, pa, pb, pc, pd, qa, qb, qc, qd, acc, out_acc,
+    grads, own_grads, r_core, s_xy, pa, pb, pc, pd, qa, qb, qc, qd, acc, out_acc,
     send, recv, load,
 ):
     arrays = (
@@ -165,8 +165,8 @@
         copy.wait()
 
     for r in range(NC):
-        grads[r * REGION + HALF:(r + 1) * REGION] = jnp.zeros((REGION - HALF, C), F32)
-    r_core[HALF:REGION] = jnp.zeros((REGION - HALF, C), F32)
+        own_grads[r * REGION + HALF:(r + 1) * REGION] = jnp.zeros((REGION - HALF, C), F32)
+    r_core[HALF:REGION] = jnp.zeros((REGION - HALF, C), BF16)
 
     own = clip[span]
     before = clip[lax.rem(span + SPANS - 1, SPANS)]
@@ -266,13 +266,15 @@
     def activate(f, carry):
         for r in range(RB + 2):
             lifted = (fp_buf[f, r].astype(F32) - mean) * lift + shift_row
-            a = lifted / (1.0 + jnp.exp(-lifted))
+            half = 0.5 * lifted
+            a = half + half * jnp.tanh(half)
             if r == 0:
                 a = a * above
             if r == RB + 1:
                 a = a * below
-            act[f, r] = a.astype(BF16)
-            flat = a.T.astype(BF16)
+            a = a.astype(BF16)
+            act[f, r] = a
+            flat = a.T
             for k in range(RB):
                 dr = r - k
                 if 0 <= dr < 3:
@@ -289,15 +291,17 @@
         for b in range(9):
             dr, ds = b // 3, b % 3
             piece = g[dr * C:(dr + 1) * C, ds * C:(ds + 1) * C]
-            if k != 1:
-                at = pl.multiple_of(t * (9 * C + 32) + b * C, 64)
-                grads[pl.ds(at, C)] = piece
-            elif b != 4:
-                at = (9 + b) * C + (REGION - HALF if b > 4 else 0)
-                grads[at:at + C] = piece
-            else:
-                grads[HALF - 64:HALF] = piece[0:64]
-                grads[REGION:REGION + 64] = piece[64:128]
+            for ref in ((grads,), (grads, own_grads), (own_grads,))[k]:
+                part = piece.astype(ref.dtype)
+                if k != 1:
+                    at = pl.multiple_of(t * (9 * C + 32) + b * C, 64)
+                    ref[pl.ds(at, C)] = part
+                elif b != 4:
+                    at = (9 + b) * C + (REGION - HALF if b > 4 else 0)
+                    ref[at:at + C] = part
+                else:
+                    ref[HALF - 64:HALF] = part[0:64]
+                    ref[REGION:REGION + 64] = part[64:128]
         if k < 2:
             size = (9 * C, HALF - 9 * C)[k]
             source = ((1 - c) * 2 * (9 * C + 32), c * 9 * C + (1 - c) * REGION)[k]
@@ -312,8 +316,8 @@
     mine = c * REGION
 
     def both_cores(at, rows):
-        a = grads[pl.ds(pl.multiple_of(mine + at, 16), rows)]
-        return (a + r_core[pl.ds(pl.multiple_of(at, 16), rows)]).astype(BF16)
+        a = own_grads[pl.ds(pl.multiple_of(mine + at, 16), rows)]
+        return (a + r_core[pl.ds(pl.multiple_of(at, 16), rows)].astype(F32)).astype(BF16)
 
     for o in PLANE_OFFS:
         px, py = lax.rem(x + o[0], NX), lax.rem(y + o[1], NY)
@@ -576,8 +580,9 @@
             pltpu.VMEM((16, C), F32),
             pltpu.VMEM((LINE, 16, C), F32),
             pltpu.VMEM((LINE, 8, C), F32),
+            pltpu.VMEM((NC * REGION, C), BF16),
             pltpu.VMEM((NC * REGION, C), F32),
-            pltpu.VMEM((REGION, C), F32),
+            pltpu.VMEM((REGION, C), BF16),
             pltpu.VMEM((REGION, C), BF16),
             pltpu.VMEM((PLANE, CHUNK_P, C), BF16),
             pltpu.VMEM((NZ, CHUNK_P, C), BF16),

time: 49.7 us -> 48.8 us (0.982)
  Pallas kernels: 48.9 us -> 48 us
    pallas_call x1, Pallas kernels: 47 us -> 46.1 us  [local(): pl.pallas_call(kernel, out_shape=(jax.ShapeDtypeStruct(frames.shape, BF16...]
where the time goes in v4:
time: 48.8 us; the launch traced here: 48.7 us
  Pallas kernels  48 us (98%)
  between operations  0.64 us (1%)
    pallas_call x1, Pallas kernels, local(): pl.pallas_call(kernel, out_shape=(jax.ShapeDtypeStruct(frames.shape, BF16...  46.1 us
    pallas_call x1, Pallas kernels, local(): pl.pallas_call(writer, out_shape=(jax.ShapeDtypeStruct(frames.shape, BF16...  1.94 us

profile of v4, /device:TPU:1, one launch (start us, length us, event | category | flops | bytes accessed | tf_op | source)
XLA Modules:
  0.0 48.7 jit_solution(8266497648559434188)
XLA Ops:
  0.6 46.1 %block.1 = (bf16[1,4,2,128,128]{4,3,2,1,0:T(8,128)(2,1)S(1)}, bf16[1,4,2,128,128]{4,3,2,1,0:T(8,128)(2,1)S(1)}, bf16[3456,128]{1,0:T(8,128)(2,1)S(1)}, f32[8,128]{1,0:T(8,128)S(1)}) custom-call(bf16[1,4,2,128,128]{4,3,2,1,0:T(8,128)(2,1)} %frames_hbm.1, bf16[1,4,2,128,128]{4,3,2,1,0:T(8,128)(2,1)} %cot_hbm.1, bf16[9,384,128]{2,1,0:T(8,128)(2,1)} %bitcast.9, ...), custom_call_target="tpu_custom_call" | custom-call | flops 3000000000 | bytes 4000000 | tf_op jit(solution)/shard_map/block/pallas_call | solution.py:549
  46.7 1.9 %writer.1 = (bf16[1,4,2,128,128]{4,3,2,1,0:T(8,128)(2,1)}, bf16[1,4,2,128,128]{4,3,2,1,0:T(8,128)(2,1)}, f32[3456,128]{1,0:T(8,128)}, f32[1,128]{1,0:T(1,128)}, f32[1,128]{1,0:T(1,128)}, /*index=5*/f32[1,128]{1,0:T(1,128)}) custom-call(bf16[1,4,2,128,128]{4,3,2,1,0:T(8,128)(2,1)S(1)} %get-tuple-element.16.enc, ...), custom_call_target="tpu_custom_call" | custom-call | tf_op jit(solution)/shard_map/writer/pallas_call | solution.py:607
